TPU v7x, 32 devices: a whole 2x2x4 slice. The times are simulated.
32 devices in a mesh: tx: 4 (over z), ty: 8 (over y, x, core).
Axes of the slice: x: 2, y: 2, z: 4, core: 2. Of those that a mesh axis runs over, the one named last changes fastest.
Arguments:
- voxels: bfloat16 [131072, 128], P(('tx', 'ty')), may hold values from 0 to 9
- owner_tile: int32 [131072, 1], P(('tx', 'ty')), may hold values from 0 to 31; in each aligned block of 4096 rows (0 to 4095, 4096 to 8191, ...) at most 256 rows name the same one
- rim_blocks: int32 [32, 4, 16], P(('tx', 'ty')), may hold values from 0 to 127
- kernel_map: int32 [32, 27, 8192], P(('tx', 'ty')), may hold values from -1 to 12287, as said below
- weights: bfloat16 [27, 128, 128], replicated, may hold values from -0.109375 to 0.109375
- norm_gain: float32 [128], replicated, may hold values from 0.1 to 1.9
- shift_bias: float32 [128], replicated, may hold values from -3 to 3
Outputs:
- normalized: bfloat16 [262144, 128], P(('tx', 'ty'))
Inputs may be any that keep to these rules, and one draw needn't show every extreme that they name: `owner_tile`: at most 256 of one device's 4096 rows name one tile, and in every draw some device's rows name some tile exactly 256 times. `kernel_map`: for each tile, offset and aligned block of 64 output slots, all entries other than -1 lie in one block of the extended rows. The middle offset maps every slot to itself.
All inputs are finite; a program needn't handle non-finite values.
Results may differ from a plain program's by a relative error of at most 0.0004.
Values may be sent and summed in bfloat16 or wider, within the bound.
A program may use at most 64 MiB of HBM per device.

v0:
```python
import jax
import jax.numpy as jnp
from jax import lax
from jax.sharding import PartitionSpec as P

BLOCK = 64


def from_behind(value, axis, steps):
    count = lax.axis_size(axis)
    leading, last = (max(0, -steps), min(count, count - steps))
    return lax.ppermute(value, axis, [(source, source + steps) for source in range(leading, last)])


def along_rows(payload, stride):
    return from_behind(payload, "tx", stride)


def along_cols(payload, stride):
    return from_behind(payload, "ty", stride)


def shards(voxels, owner_tile, rim_blocks, kernel_map, weights, norm_gain, shift_bias):
    devices = lax.axis_size(("tx", "ty"))
    src_count = voxels.shape[0]
    channels = voxels.shape[1]
    tile_rows = kernel_map.shape[2]
    pair_rows = tile_rows // devices
    target = owner_tile[:, 0]
    member = (target[:, None] == jnp.arange(devices, dtype=jnp.int32)[None, :]).astype(jnp.bfloat16)
    run_len = min(512, src_count)
    run_count = src_count // run_len
    member_runs = member.reshape(run_count, run_len, devices)
    lower_ones = (jnp.arange(run_len)[:, None] >= jnp.arange(run_len)[None, :]).astype(jnp.bfloat16)
    inside = jnp.einsum("ij,bjd->bid", lower_ones, member_runs, preferred_element_type=jnp.float32)
    run_totals = inside[:, -1, :]
    before = jnp.cumsum(run_totals, axis=0) - run_totals
    running = (inside + before[:, None, :]).reshape(src_count, devices)
    member_wide = member.astype(jnp.float32)
    placed = jnp.sum((running - 1.0) * member_wide, axis=1).astype(jnp.int32)
    address = target * pair_rows + placed
    filled = jnp.sum(member_wide, axis=0).astype(jnp.bfloat16)
    slot_len = min(512, tile_rows)

    def place_slots(first):
        slots = first * slot_len + jnp.arange(slot_len, dtype=jnp.int32)
        chooser = (slots[:, None] == address[None, :]).astype(jnp.bfloat16)
        return jnp.dot(chooser, voxels, preferred_element_type=jnp.float32).astype(jnp.bfloat16)

    outgoing = lax.map(place_slots, jnp.arange(tile_rows // slot_len, dtype=jnp.int32)).reshape(
        tile_rows, channels
    )
    arrival, received = (
        lax.all_to_all(
            outgoing.reshape(devices, pair_rows, channels),
            ("tx", "ty"),
            split_axis=0,
            concat_axis=0,
            tiled=True,
        ),
        lax.all_to_all(
            filled.reshape(devices, 1), ("tx", "ty"), split_axis=0, concat_axis=0, tiled=True
        ),
    )
    arrival = arrival.reshape(tile_rows, channels)
    occupied = jnp.arange(pair_rows, dtype=jnp.float32)[None, :] < received.astype(jnp.float32)
    occupied = occupied.astype(jnp.float32).reshape(tile_rows)
    blocked = arrival.reshape(tile_rows // BLOCK, BLOCK, channels)
    picked = blocked[rim_blocks[0]]
    lower_x = along_rows(picked[0], 1)
    upper_x = along_rows(picked[1], -1)
    lower_y = along_cols(picked[2], 1)
    upper_y = along_cols(picked[3], -1)
    margin = jnp.concatenate((lower_x, upper_x, lower_y, upper_y), axis=0).reshape(-1, channels)
    extended = jnp.concatenate((arrival, margin), axis=0)
    ext_blocks = extended.reshape(-1, BLOCK, channels)
    offsets = kernel_map.shape[1]
    out_blocks = tile_rows // BLOCK
    block_map = kernel_map[0].reshape(offsets, out_blocks, BLOCK)
    source_block = jnp.maximum(jnp.max(block_map, axis=2) // BLOCK, 0)
    local_row = block_map - source_block[:, :, None] * BLOCK
    window = min(512, tile_rows)
    per_window = window // BLOCK
    windows = tile_rows // window
    source_groups = source_block.reshape(offsets, windows, per_window).transpose(1, 0, 2)
    local_groups = local_row.reshape(offsets, windows, per_window, BLOCK).transpose(1, 0, 2, 3)
    valid_groups = (
        (block_map >= 0).reshape(offsets, windows, per_window, BLOCK).transpose(1, 0, 2, 3)
    )
    positions = jnp.arange(BLOCK, dtype=jnp.int32)

    def convolve(bundle):
        sources, locals_here, valid_here = bundle
        fetched = ext_blocks[sources]
        selector = ((locals_here[..., None] == positions) & valid_here[..., None]).astype(
            jnp.bfloat16
        )
        chosen = jnp.einsum(
            "kbrj,kbjc->kbrc", selector, fetched, preferred_element_type=jnp.float32
        ).astype(jnp.bfloat16)
        return jnp.einsum("kbrc,kco->bro", chosen, weights, preferred_element_type=jnp.float32)

    response = (
        lax.map(convolve, (source_groups, local_groups, valid_groups)).reshape(tile_rows, -1)
        * occupied[:, None]
    )
    population = jnp.float32(voxels.shape[0] * devices)
    average = lax.psum(jnp.sum(response, axis=0), ("tx", "ty")) / population
    centred = (response - average) * occupied[:, None]
    variance = lax.psum(jnp.sum(centred * centred, axis=0), ("tx", "ty")) / population
    scaled = norm_gain * (response - average) / jnp.sqrt(variance + 1e-05) + shift_bias
    return (jnp.maximum(scaled, 0.0) * occupied[:, None]).astype(jnp.bfloat16)


def solution(mesh):
    return jax.shard_map(
        shards,
        mesh=mesh,
        in_specs=(
            P(("tx", "ty"), None),
            P(("tx", "ty"), None),
            P(("tx", "ty"), None, None),
            P(("tx", "ty"), None, None),
            P(),
            P(),
            P(),
        ),
        out_specs=P(("tx", "ty"), None),
        check_vma=False,
    )
```

profile of v0, /device:TPU:0, one launch (start us, length us, event | category | flops | bytes accessed | tf_op | source)
XLA Modules:
  0.0 454.8 jit_solution(17145657777077643697)
XLA Ops:
  1.6 7.3 %all-to-all-start.1 = ((bf16[32,1,1]{2,1,0:T(2,128)(2,1)}), bf16[32,1,1]{2,1,0:T(2,128)(2,1)S(1)}, u32[]{:S(2)}, u32[]{:S(2)}) async-start(bf16[32,1,1]{2,1,0:T(2,128)(2,1)} %copy.47), calls=%async_computation.1 | async-start | bytes 32768 | tf_op jit(solution)/shard_map/all_to_all | solution.py:61
  12.4 71.2 %while.21 = (s32[]{:T(128)}, bf16[16,512,128]{2,1,0:T(8,128)(2,1)}, s32[16]{0:T(128)S(1)}, s32[4096]{0:T(1024)S(1)}, bf16[4096,128]{1,0:T(8,128)(2,1)}, /*index=5*/s32[]{:T(128)}, s32[1]{0:T(128)}) while((s32[]{:T(128)}, bf16[16,512,128]{2,1,0:T(8,128)(2,1)}, s32[16]{0:T(128)S(1)}, s32[4096]{0:T(1024)S(1)}, bf16[4096,128]{1,0:T(8,128)(2,1)}, ...), condition=%wide.region_4.5_spmd, body=%wide.region_3.4_spmd.sunk | while | flops 539034112 | bytes 1200745 | solution.py:50
  13.6 3.2 fusion.78
  27.0 3.2 fusion.78
  31.4 3.2 fusion.78
  53.7 3.2 fusion.78
  71.5 3.2 fusion.78
  80.4 3.2 fusion.78
  83.6 6.0 %all-to-all-start = ((bf16[32,256,128]{2,1,0:T(8,128)(2,1)}), bf16[32,256,128]{2,1,0:T(8,128)(2,1)}, u32[]{:S(2)}, u32[]{:S(2)}) async-start(bf16[32,256,128]{2,1,0:T(8,128)(2,1)} %bitcast.9), calls=%async_computation | async-start | bytes 4194304 | tf_op jit(solution)/shard_map/all_to_all | solution.py:54
  99.9 38.5 %all-to-all-done = bf16[32,256,128]{2,1,0:T(8,128)(2,1)} async-done(((bf16[32,256,128]{2,1,0:T(8,128)(2,1)}), bf16[32,256,128]{2,1,0:T(8,128)(2,1)}, u32[]{:S(2)}, u32[]{:S(2)}) %all-to-all-start) | async-done | bytes 2097184 | tf_op jit(solution)/shard_map/all_to_all | solution.py:54
  148.6 4.1 collective-permute-done.1
  152.9 7.4 %pad_maximum_fusion = bf16[12288,128]{1,0:T(8,128)(2,1)S(1)} fusion(bf16[4096,128]{1,0:T(8,128)(2,1)S(1)} %bitcast.112, bf16[8192,128]{1,0:T(8,128)(2,1)} %bitcast.10), kind=kLoop, calls=%fused_computation.39 | loop fusion | flops 6291456 | bytes 6291456 | tf_op jit(solution)/shard_map/concatenate | solution.py:75
  160.3 200.1 %while.22 = (s32[]{:T(128)}, f32[16,8,64,128]{3,2,1,0:T(8,128)}, s32[16,27,8,64]{3,2,0,1:T(8,128)}, pred[16,27,8,64]{3,2,0,1:T(8,128)(4,1)}, s32[16,27,8]{1,2,0:...) while((s32[]{:T(128)}, f32[16,8,64,128]{3,2,1,0:T(8,128)}, ...), condition=%wide.region_6.7_spmd.clone, body=%wide.region_5.6_spmd.clone.sunk | while | flops 683017856 | bytes 12122657 | solution.py:104
  165.1 7.7 %fusion.83 = f32[16,8,64,128]{3,2,1,0:T(8,128)} fusion(f32[16,8,64,128]{3,2,1,0:T(8,128)} %get-tuple-element.261, s32[]{:T(128)} %get-tuple-element.260, bf16[27,8,64,128]{3,2,1,0:T(8,128)(2,1)} %bitcast.111, s32[27,8,64]{2,0,1:T(8,128)S(1)} %bitcast.113, pred[27,8,64]{2,0,1:T(8,128)(4,1)S(1)} %bitcast.114, bf16[27,128,128]{2,1,0:T(8,128)(2,1)} %get-tuple-element.274), kind=kOutput, calls=%fused_computation.20.clone.1 | convolution fusion | flops 683016192 | bytes 4755456 | tf_op jit(solution)/shard_map/while/body/eval_jaxpr/kbrc,kco->bro/dot_general | solution.py:101
  177.6 7.7 %fusion.83 = f32[16,8,64,128]{3,2,1,0:T(8,128)} fusion(f32[16,8,64,128]{3,2,1,0:T(8,128)} %get-tuple-element.261, s32[]{:T(128)} %get-tuple-element.260, bf16[27,8,64,128]{3,2,1,0:T(8,128)(2,1)} %bitcast.111, s32[27,8,64]{2,0,1:T(8,128)S(1)} %bitcast.113, pred[27,8,64]{2,0,1:T(8,128)(4,1)S(1)} %bitcast.114, bf16[27,128,128]{2,1,0:T(8,128)(2,1)} %get-tuple-element.274), kind=kOutput, calls=%fused_computation.20.clone.1 | convolution fusion | flops 683016192 | bytes 4755456 | tf_op jit(solution)/shard_map/while/body/eval_jaxpr/kbrc,kco->bro/dot_general | solution.py:101
  190.1 7.7 %fusion.83 = f32[16,8,64,128]{3,2,1,0:T(8,128)} fusion(f32[16,8,64,128]{3,2,1,0:T(8,128)} %get-tuple-element.261, s32[]{:T(128)} %get-tuple-element.260, bf16[27,8,64,128]{3,2,1,0:T(8,128)(2,1)} %bitcast.111, s32[27,8,64]{2,0,1:T(8,128)S(1)} %bitcast.113, pred[27,8,64]{2,0,1:T(8,128)(4,1)S(1)} %bitcast.114, bf16[27,128,128]{2,1,0:T(8,128)(2,1)} %get-tuple-element.274), kind=kOutput, calls=%fused_computation.20.clone.1 | convolution fusion | flops 683016192 | bytes 4755456 | tf_op jit(solution)/shard_map/while/body/eval_jaxpr/kbrc,kco->bro/dot_general | solution.py:101
  202.6 7.7 %fusion.83 = f32[16,8,64,128]{3,2,1,0:T(8,128)} fusion(f32[16,8,64,128]{3,2,1,0:T(8,128)} %get-tuple-element.261, s32[]{:T(128)} %get-tuple-element.260, bf16[27,8,64,128]{3,2,1,0:T(8,128)(2,1)} %bitcast.111, s32[27,8,64]{2,0,1:T(8,128)S(1)} %bitcast.113, pred[27,8,64]{2,0,1:T(8,128)(4,1)S(1)} %bitcast.114, bf16[27,128,128]{2,1,0:T(8,128)(2,1)} %get-tuple-element.274), kind=kOutput, calls=%fused_computation.20.clone.1 | convolution fusion | flops 683016192 | bytes 4755456 | tf_op jit(solution)/shard_map/while/body/eval_jaxpr/kbrc,kco->bro/dot_general | solution.py:101
  215.1 7.7 %fusion.83 = f32[16,8,64,128]{3,2,1,0:T(8,128)} fusion(f32[16,8,64,128]{3,2,1,0:T(8,128)} %get-tuple-element.261, s32[]{:T(128)} %get-tuple-element.260, bf16[27,8,64,128]{3,2,1,0:T(8,128)(2,1)} %bitcast.111, s32[27,8,64]{2,0,1:T(8,128)S(1)} %bitcast.113, pred[27,8,64]{2,0,1:T(8,128)(4,1)S(1)} %bitcast.114, bf16[27,128,128]{2,1,0:T(8,128)(2,1)} %get-tuple-element.274), kind=kOutput, calls=%fused_computation.20.clone.1 | convolution fusion | flops 683016192 | bytes 4755456 | tf_op jit(solution)/shard_map/while/body/eval_jaxpr/kbrc,kco->bro/dot_general | solution.py:101
  227.6 7.7 %fusion.83 = f32[16,8,64,128]{3,2,1,0:T(8,128)} fusion(f32[16,8,64,128]{3,2,1,0:T(8,128)} %get-tuple-element.261, s32[]{:T(128)} %get-tuple-element.260, bf16[27,8,64,128]{3,2,1,0:T(8,128)(2,1)} %bitcast.111, s32[27,8,64]{2,0,1:T(8,128)S(1)} %bitcast.113, pred[27,8,64]{2,0,1:T(8,128)(4,1)S(1)} %bitcast.114, bf16[27,128,128]{2,1,0:T(8,128)(2,1)} %get-tuple-element.274), kind=kOutput, calls=%fused_computation.20.clone.1 | convolution fusion | flops 683016192 | bytes 4755456 | tf_op jit(solution)/shard_map/while/body/eval_jaxpr/kbrc,kco->bro/dot_general | solution.py:101
  240.1 7.7 %fusion.83 = f32[16,8,64,128]{3,2,1,0:T(8,128)} fusion(f32[16,8,64,128]{3,2,1,0:T(8,128)} %get-tuple-element.261, s32[]{:T(128)} %get-tuple-element.260, bf16[27,8,64,128]{3,2,1,0:T(8,128)(2,1)} %bitcast.111, s32[27,8,64]{2,0,1:T(8,128)S(1)} %bitcast.113, pred[27,8,64]{2,0,1:T(8,128)(4,1)S(1)} %bitcast.114, bf16[27,128,128]{2,1,0:T(8,128)(2,1)} %get-tuple-element.274), kind=kOutput, calls=%fused_computation.20.clone.1 | convolution fusion | flops 683016192 | bytes 4755456 | tf_op jit(solution)/shard_map/while/body/eval_jaxpr/kbrc,kco->bro/dot_general | solution.py:101
  252.6 7.7 %fusion.83 = f32[16,8,64,128]{3,2,1,0:T(8,128)} fusion(f32[16,8,64,128]{3,2,1,0:T(8,128)} %get-tuple-element.261, s32[]{:T(128)} %get-tuple-element.260, bf16[27,8,64,128]{3,2,1,0:T(8,128)(2,1)} %bitcast.111, s32[27,8,64]{2,0,1:T(8,128)S(1)} %bitcast.113, pred[27,8,64]{2,0,1:T(8,128)(4,1)S(1)} %bitcast.114, bf16[27,128,128]{2,1,0:T(8,128)(2,1)} %get-tuple-element.274), kind=kOutput, calls=%fused_computation.20.clone.1 | convolution fusion | flops 683016192 | bytes 4755456 | tf_op jit(solution)/shard_map/while/body/eval_jaxpr/kbrc,kco->bro/dot_general | solution.py:101
  265.1 7.7 %fusion.83 = f32[16,8,64,128]{3,2,1,0:T(8,128)} fusion(f32[16,8,64,128]{3,2,1,0:T(8,128)} %get-tuple-element.261, s32[]{:T(128)} %get-tuple-element.260, bf16[27,8,64,128]{3,2,1,0:T(8,128)(2,1)} %bitcast.111, s32[27,8,64]{2,0,1:T(8,128)S(1)} %bitcast.113, pred[27,8,64]{2,0,1:T(8,128)(4,1)S(1)} %bitcast.114, bf16[27,128,128]{2,1,0:T(8,128)(2,1)} %get-tuple-element.274), kind=kOutput, calls=%fused_computation.20.clone.1 | convolution fusion | flops 683016192 | bytes 4755456 | tf_op jit(solution)/shard_map/while/body/eval_jaxpr/kbrc,kco->bro/dot_general | solution.py:101
  277.7 7.7 %fusion.83 = f32[16,8,64,128]{3,2,1,0:T(8,128)} fusion(f32[16,8,64,128]{3,2,1,0:T(8,128)} %get-tuple-element.261, s32[]{:T(128)} %get-tuple-element.260, bf16[27,8,64,128]{3,2,1,0:T(8,128)(2,1)} %bitcast.111, s32[27,8,64]{2,0,1:T(8,128)S(1)} %bitcast.113, pred[27,8,64]{2,0,1:T(8,128)(4,1)S(1)} %bitcast.114, bf16[27,128,128]{2,1,0:T(8,128)(2,1)} %get-tuple-element.274), kind=kOutput, calls=%fused_computation.20.clone.1 | convolution fusion | flops 683016192 | bytes 4755456 | tf_op jit(solution)/shard_map/while/body/eval_jaxpr/kbrc,kco->bro/dot_general | solution.py:101
  290.1 7.7 %fusion.83 = f32[16,8,64,128]{3,2,1,0:T(8,128)} fusion(f32[16,8,64,128]{3,2,1,0:T(8,128)} %get-tuple-element.261, s32[]{:T(128)} %get-tuple-element.260, bf16[27,8,64,128]{3,2,1,0:T(8,128)(2,1)} %bitcast.111, s32[27,8,64]{2,0,1:T(8,128)S(1)} %bitcast.113, pred[27,8,64]{2,0,1:T(8,128)(4,1)S(1)} %bitcast.114, bf16[27,128,128]{2,1,0:T(8,128)(2,1)} %get-tuple-element.274), kind=kOutput, calls=%fused_computation.20.clone.1 | convolution fusion | flops 683016192 | bytes 4755456 | tf_op jit(solution)/shard_map/while/body/eval_jaxpr/kbrc,kco->bro/dot_general | solution.py:101
  302.6 7.7 %fusion.83 = f32[16,8,64,128]{3,2,1,0:T(8,128)} fusion(f32[16,8,64,128]{3,2,1,0:T(8,128)} %get-tuple-element.261, s32[]{:T(128)} %get-tuple-element.260, bf16[27,8,64,128]{3,2,1,0:T(8,128)(2,1)} %bitcast.111, s32[27,8,64]{2,0,1:T(8,128)S(1)} %bitcast.113, pred[27,8,64]{2,0,1:T(8,128)(4,1)S(1)} %bitcast.114, bf16[27,128,128]{2,1,0:T(8,128)(2,1)} %get-tuple-element.274), kind=kOutput, calls=%fused_computation.20.clone.1 | convolution fusion | flops 683016192 | bytes 4755456 | tf_op jit(solution)/shard_map/while/body/eval_jaxpr/kbrc,kco->bro/dot_general | solution.py:101
  315.2 7.7 %fusion.83 = f32[16,8,64,128]{3,2,1,0:T(8,128)} fusion(f32[16,8,64,128]{3,2,1,0:T(8,128)} %get-tuple-element.261, s32[]{:T(128)} %get-tuple-element.260, bf16[27,8,64,128]{3,2,1,0:T(8,128)(2,1)} %bitcast.111, s32[27,8,64]{2,0,1:T(8,128)S(1)} %bitcast.113, pred[27,8,64]{2,0,1:T(8,128)(4,1)S(1)} %bitcast.114, bf16[27,128,128]{2,1,0:T(8,128)(2,1)} %get-tuple-element.274), kind=kOutput, calls=%fused_computation.20.clone.1 | convolution fusion | flops 683016192 | bytes 4755456 | tf_op jit(solution)/shard_map/while/body/eval_jaxpr/kbrc,kco->bro/dot_general | solution.py:101
  327.7 7.7 %fusion.83 = f32[16,8,64,128]{3,2,1,0:T(8,128)} fusion(f32[16,8,64,128]{3,2,1,0:T(8,128)} %get-tuple-element.261, s32[]{:T(128)} %get-tuple-element.260, bf16[27,8,64,128]{3,2,1,0:T(8,128)(2,1)} %bitcast.111, s32[27,8,64]{2,0,1:T(8,128)S(1)} %bitcast.113, pred[27,8,64]{2,0,1:T(8,128)(4,1)S(1)} %bitcast.114, bf16[27,128,128]{2,1,0:T(8,128)(2,1)} %get-tuple-element.274), kind=kOutput, calls=%fused_computation.20.clone.1 | convolution fusion | flops 683016192 | bytes 4755456 | tf_op jit(solution)/shard_map/while/body/eval_jaxpr/kbrc,kco->bro/dot_general | solution.py:101
  340.2 7.7 %fusion.83 = f32[16,8,64,128]{3,2,1,0:T(8,128)} fusion(f32[16,8,64,128]{3,2,1,0:T(8,128)} %get-tuple-element.261, s32[]{:T(128)} %get-tuple-element.260, bf16[27,8,64,128]{3,2,1,0:T(8,128)(2,1)} %bitcast.111, s32[27,8,64]{2,0,1:T(8,128)S(1)} %bitcast.113, pred[27,8,64]{2,0,1:T(8,128)(4,1)S(1)} %bitcast.114, bf16[27,128,128]{2,1,0:T(8,128)(2,1)} %get-tuple-element.274), kind=kOutput, calls=%fused_computation.20.clone.1 | convolution fusion | flops 683016192 | bytes 4755456 | tf_op jit(solution)/shard_map/while/body/eval_jaxpr/kbrc,kco->bro/dot_general | solution.py:101
  352.7 7.7 %fusion.83 = f32[16,8,64,128]{3,2,1,0:T(8,128)} fusion(f32[16,8,64,128]{3,2,1,0:T(8,128)} %get-tuple-element.261, s32[]{:T(128)} %get-tuple-element.260, bf16[27,8,64,128]{3,2,1,0:T(8,128)(2,1)} %bitcast.111, s32[27,8,64]{2,0,1:T(8,128)S(1)} %bitcast.113, pred[27,8,64]{2,0,1:T(8,128)(4,1)S(1)} %bitcast.114, bf16[27,128,128]{2,1,0:T(8,128)(2,1)} %get-tuple-element.274), kind=kOutput, calls=%fused_computation.20.clone.1 | convolution fusion | flops 683016192 | bytes 4755456 | tf_op jit(solution)/shard_map/while/body/eval_jaxpr/kbrc,kco->bro/dot_general | solution.py:101
  363.3 42.7 %psum.14 = f32[128]{0:T(128)S(1)} all-reduce(f32[128]{0:T(128)S(1)} %multiply_reduce_fusion.1), channel_id=1, replica_groups=mesh['tx'=4,'ty'=8] {'tx','ty'}, use_global_device_ids=true, to_apply=%region_9.10 | all-reduce | flops 128 | bytes 1024 | tf_op jit(solution)/shard_map/psum | solution.py:108
  408.8 39.8 %psum.15 = f32[128]{0:T(128)S(1)} all-reduce(f32[128]{0:T(128)S(1)} %multiply_reduce_fusion), channel_id=1, replica_groups=mesh['tx'=4,'ty'=8] {'tx','ty'}, use_global_device_ids=true, to_apply=%region_11.12 | all-reduce | flops 128 | bytes 1024 | tf_op jit(solution)/shard_map/psum | solution.py:110
  448.6 6.1 %fusion.52 = bf16[8192,128]{1,0:T(8,128)(2,1)} fusion(f32[16,8,64,128]{3,2,1,0:T(8,128)} %get-tuple-element.75, f32[128]{0:T(128)S(1)} %copy-done.2, f32[128]{0:T(128)S(1)} %add_sqrt_fusion, f32[128]{0:T(128)S(1)} %broadcast_multiply_fusion.1, f32[8192]{0:T(1024)S(1)} %bitcast.117, f32[128]{0:T(128)S(1)} %copy-done.3), kind=kLoop, calls=%fused_computation.37 | loop fusion | flops 8388608 | bytes 6326272 | tf_op jit(solution)/shard_map/convert_element_type | solution.py:112
  (261 shorter events, 149.3 us)
Async XLA Ops:
  1.6 82.0 %all-to-all-start.1 = ((bf16[32,1,1]{2,1,0:T(2,128)(2,1)}), bf16[32,1,1]{2,1,0:T(2,128)(2,1)S(1)}, u32[]{:S(2)}, u32[]{:S(2)}) async-start(bf16[32,1,1]{2,1,0:T(2,128)(2,1)} %copy.47), calls=%async_computation.1 | async-start | bytes 32768 | tf_op jit(solution)/shard_map/all_to_all | solution.py:61
  83.6 6.0 %copy-start = (s32[1,27,8192]{2,0,1:T(1,128)S(1)}, s32[1,27,8192]{2,0,1:T(1,128)}, u32[]{:S(2)}) copy-start(s32[1,27,8192]{2,0,1:T(1,128)} %param.14) | copy-start | bytes 2654212
  83.6 54.8 %all-to-all-start = ((bf16[32,256,128]{2,1,0:T(8,128)(2,1)}), bf16[32,256,128]{2,1,0:T(8,128)(2,1)}, u32[]{:S(2)}, u32[]{:S(2)}) async-start(bf16[32,256,128]{2,1,0:T(8,128)(2,1)} %bitcast.9), calls=%async_computation | async-start | bytes 4194304 | tf_op jit(solution)/shard_map/all_to_all | solution.py:54
  89.5 4.8 %copy-start.1 = (s32[1,4,16]{2,1,0:T(4,128)S(1)}, s32[1,4,16]{2,1,0:T(4,128)}, u32[]{:S(2)}) copy-start(s32[1,4,16]{2,1,0:T(4,128)} %param.13) | copy-start | bytes 772
  140.8 7.8 %collective-permute-start = (bf16[16,64,128]{2,1,0:T(8,128)(2,1)S(1)}, bf16[16,64,128]{2,1,0:T(8,128)(2,1)S(1)}, u32[]{:S(2)}, u32[]{:S(2)}) collective-permute-start(bf16[16,64,128]{2,1,0:T(8,128)(2,1)S(1)} %get-tuple-element.151), channel_id=1, source_target_pairs={{0,8},{8,16},{16,24},{1,9},{9,17},{17,25},{2,10},{10,18},{18,26},{... | collective-permute-start | bytes 786440 | tf_op jit(solution)/shard_map/ppermute | solution.py:12
  142.3 10.5 %collective-permute-start.1 = (bf16[16,64,128]{2,1,0:T(8,128)(2,1)S(1)}, bf16[16,64,128]{2,1,0:T(8,128)(2,1)S(1)}, u32[]{:S(2)}, u32[]{:S(2)}) collective-permute-start(bf16[16,64,128]{2,1,0:T(8,128)(2,1)S(1)} %get-tuple-element.153), channel_id=1, source_target_pairs={{8,0},{16,8},{24,16},{9,1},{17,9},{25,17},{10,2},{18,10},{26,18},{... | collective-permute-start | bytes 786440 | tf_op jit(solution)/shard_map/ppermute | solution.py:12
  143.6 9.2 %collective-permute-start.2 = (bf16[16,64,128]{2,1,0:T(8,128)(2,1)S(1)}, bf16[16,64,128]{2,1,0:T(8,128)(2,1)S(1)}, u32[]{:S(2)}, u32[]{:S(2)}) collective-permute-start(bf16[16,64,128]{2,1,0:T(8,128)(2,1)S(1)} %get-tuple-element.152), channel_id=1, source_target_pairs={{0,1},{1,2},{2,3},{3,4},{4,5},{5,6},{6,7},{8,9},{9,10},{10,11},{11... | collective-permute-start | bytes 786440 | tf_op jit(solution)/shard_map/ppermute | solution.py:12
  145.9 6.9 %collective-permute-start.3 = (bf16[16,64,128]{2,1,0:T(8,128)(2,1)S(1)}, bf16[16,64,128]{2,1,0:T(8,128)(2,1)S(1)}, u32[]{:S(2)}, u32[]{:S(2)}) collective-permute-start(bf16[16,64,128]{2,1,0:T(8,128)(2,1)S(1)} %get-tuple-element.154), channel_id=1, source_target_pairs={{1,0},{2,1},{3,2},{4,3},{5,4},{6,5},{7,6},{9,8},{10,9},{11,10},{12... | collective-permute-start | bytes 786440 | tf_op jit(solution)/shard_map/ppermute | solution.py:12
  360.4 88.3 %copy-start.2 = (f32[128]{0:T(128)S(1)}, f32[128]{0:T(128)}, u32[]{:S(2)}) copy-start(f32[128]{0:T(128)} %param.17) | copy-start | bytes 1540
  360.4 88.3 %copy-start.3 = (f32[128]{0:T(128)S(1)}, f32[128]{0:T(128)}, u32[]{:S(2)}) copy-start(f32[128]{0:T(128)} %param.16) | copy-start | bytes 1540
where the time goes:
time: 458 us; the launch traced here: 455 us
  matrix products  175 us (38%)
  local copies, waits for them, and re-layouts  92.9 us (20%)
  blocking collectives  82.5 us (18%)
  waiting for transfers between devices  43.5 us (9%)
  other arithmetic  30.4 us (7%)
  starting transfers between devices  19.8 us (4%)
  loops' own time  10.7 us (2%)
    dot_general x16, matrix products, convolve(): jnp.einsum('kbrc,kco->bro', chosen, weights, preferred_element_type=jnp.f...  123 us
    dot_general x16, matrix products, place_slots(): jnp.dot(chooser, voxels, preferred_element_type=jnp.float32)  51 us
    gather x16, local copies, waits for them, and re-layouts, convolve(): fetched = ext_blocks[sources]  46 us
    psum x1, blocking collectives, shards(): average = lax.psum(jnp.sum(response, axis=0), ('tx', 'ty')) / population  42.7 us
    psum x1, blocking collectives, shards(): lax.psum(jnp.sum(centred * centred, axis=0), ('tx', 'ty')) / population  39.8 us
    all_to_all x1, waiting for transfers between devices, shards(): lax.all_to_all(outgoing.reshape(devices, pair_rows, channels), ('tx', 'ty...  38.5 us
    dynamic_slice x96, local copies, waits for them, and re-layouts, shards(): lax.map(convolve, (source_groups, local_groups, valid_groups))  28.7 us
    another operation x1, loops' own time, shards(): lax.map(place_slots, jnp.arange(tile_rows // slot_len, dtype=jnp.int32))  10.4 us
  transfers between devices with their start and end apart: 6, of which 3 were waited for; matrix products, arithmetic and copies ran while one was open for 16% of the time, Pallas kernels for 0%

commit v1 on v0

v1 whole, which is shorter than its diff:
```python
import functools
import jax
import jax.numpy as jnp
from jax import lax
from jax.experimental import pallas as pl
from jax.experimental.pallas import tpu as pltpu
from jax.sharding import PartitionSpec as P

BLOCK = 64
GROUP = 8
MESH = pl.DeviceIdType.MESH


def from_behind(value, axis, steps):
    count = lax.axis_size(axis)
    leading, last = (max(0, -steps), min(count, count - steps))
    return lax.ppermute(value, axis, [(source, source + steps) for source in range(leading, last)])


def place_kernel(address_ref, voxels_ref, out_ref, wide, slots):
    rows = voxels_ref.shape[0]
    total = out_ref.shape[0]
    chunk = 256

    def widen(i, carry):
        at = pl.ds(pl.multiple_of(i * chunk, chunk), chunk)
        wide[at, :] = voxels_ref[at, :].astype(jnp.float32)
        return carry

    def clear(i, carry):
        at = pl.ds(pl.multiple_of(i * chunk, chunk), chunk)
        slots[at, :] = jnp.full((chunk, slots.shape[1]), -1.0, jnp.float32)
        return carry

    def put(i, carry):
        base = pl.multiple_of(i * 16, 16)
        for u in range(16):
            slots[pl.ds(address_ref[base + u], 1), :] = wide[pl.ds(base + u, 1), :]
        return carry

    def narrow(i, carry):
        at = pl.ds(pl.multiple_of(i * chunk, chunk), chunk)
        out_ref[at, :] = slots[at, :].astype(jnp.bfloat16)
        return carry

    lax.fori_loop(0, rows // chunk, widen, 0)
    lax.fori_loop(0, total // chunk, clear, 0)
    lax.fori_loop(0, rows // 16, put, 0)
    lax.fori_loop(0, total // chunk, narrow, 0)


def place(address, voxels, tile_rows):
    rows, channels = voxels.shape
    return pl.pallas_call(
        place_kernel,
        out_shape=jax.ShapeDtypeStruct((tile_rows, channels), jnp.bfloat16),
        in_specs=[
            pl.BlockSpec(memory_space=pltpu.SMEM),
            pl.BlockSpec(memory_space=pltpu.VMEM),
        ],
        out_specs=pl.BlockSpec(memory_space=pltpu.VMEM),
        scratch_shapes=[
            pltpu.VMEM((rows, channels), jnp.float32),
            pltpu.VMEM((tile_rows, channels), jnp.float32),
        ],
        compiler_params=pltpu.CompilerParams(vmem_limit_bytes=32 * 1024 * 1024),
    )(address, voxels)


def conv_kernel(
    sources_ref, used_ref, arrival_ref, lx_ref, ux_ref, ly_ref, uy_ref, local_ref, expand_ref,
    weights_ref, resp_ref, stats_ref, ext, chosen, listed
):
    blocks = arrival_ref.shape[0]
    rim = lx_ref.shape[0]
    pairs = expand_ref.shape[1] // 128
    offsets = 2 * pairs
    channels = arrival_ref.shape[2]
    zero16 = jnp.zeros((BLOCK, channels), jnp.bfloat16)

    def clean(i, carry):
        ext[i] = jnp.maximum(arrival_ref[i], zero16)
        resp_ref[i] = jnp.zeros((BLOCK, channels), jnp.float32)
        return carry

    def clean_rim(i, carry):
        for number, ref in enumerate((lx_ref, ux_ref, ly_ref, uy_ref)):
            ext[blocks + number * rim + i] = jnp.maximum(ref[i], zero16)
        return carry

    lax.fori_loop(0, blocks, clean, 0, unroll=4)
    lax.fori_loop(0, rim, clean_rim, 0)

    def note(b, count):
        taken = used_ref[b]
        listed[count] = b
        return count + taken

    count = lax.fori_loop(0, blocks, note, jnp.int32(0))
    for u in range(GROUP):
        listed[count + u] = listed[jnp.maximum(count - 1, 0)]
    lane = lax.broadcasted_iota(jnp.int32, (1, 128), 1)
    wanted = (lane % BLOCK).astype(jnp.float32)

    def window(w, carry):
        ids = [listed[w * GROUP + u] for u in range(GROUP)]
        local = jnp.concatenate([local_ref[b] for b in ids], axis=0)
        for p in range(pairs):
            spread = jnp.dot(
                local, expand_ref[:, p * 128 : (p + 1) * 128], preferred_element_type=jnp.float32
            )
            selector = jnp.where(spread == wanted, 1.0, 0.0).astype(jnp.bfloat16)
            for u in range(GROUP):
                first = ext[sources_ref[ids[u] * offsets + 2 * p]]
                second = ext[sources_ref[ids[u] * offsets + 2 * p + 1]]
                both = jnp.concatenate(
                    (
                        jnp.concatenate((first, zero16), axis=1),
                        jnp.concatenate((zero16, second), axis=1),
                    ),
                    axis=0,
                )
                picked = jnp.dot(
                    selector[u * BLOCK : (u + 1) * BLOCK], both, preferred_element_type=jnp.float32
                )
                chosen[u * BLOCK : (u + 1) * BLOCK, p * 256 : (p + 1) * 256] = picked.astype(
                    jnp.bfloat16
                )
        for u in range(GROUP):
            chosen[u * BLOCK : (u + 1) * BLOCK, pairs * 256 :] = ext[ids[u]]
        result = jnp.dot(chosen[...], weights_ref[...], preferred_element_type=jnp.float32)
        for u in range(GROUP):
            full = arrival_ref[ids[u]].astype(jnp.float32) >= 0.0
            resp_ref[ids[u]] = jnp.where(full, result[u * BLOCK : (u + 1) * BLOCK], 0.0)
        return carry

    lax.fori_loop(0, (count + GROUP - 1) // GROUP, window, 0)

    def add(i, carry):
        total, number = carry
        full = jnp.where(arrival_ref[i].astype(jnp.float32) >= 0.0, 1.0, 0.0)
        return (
            total + jnp.sum(resp_ref[i].reshape(BLOCK // 8, 8, channels), axis=0),
            number + jnp.sum(full.reshape(BLOCK // 8, 8, channels), axis=0),
        )

    nothing = jnp.zeros((8, channels), jnp.float32)
    total, number = lax.fori_loop(0, blocks, add, (nothing, nothing), unroll=4)
    total = jnp.sum(total, axis=0, keepdims=True)
    number = jnp.sum(number, axis=0, keepdims=True)
    mean = total / jnp.maximum(number, 1.0)

    def spread_of(i, squares):
        full = arrival_ref[i].astype(jnp.float32) >= 0.0
        off = jnp.where(full, resp_ref[i] - mean, 0.0)
        return squares + jnp.sum((off * off).reshape(BLOCK // 8, 8, channels), axis=0)

    squares = lax.fori_loop(0, blocks, spread_of, nothing, unroll=4)
    squares = jnp.sum(squares, axis=0, keepdims=True)
    row = lax.broadcasted_iota(jnp.int32, (8, channels), 0)
    stats_ref[...] = jnp.where(
        row == 0, total, jnp.where(row == 1, squares, jnp.where(row == 2, number, mean))
    )


def convolve(sources, used, arrival, rims, local, expand, weights):
    blocks, _, channels = arrival.shape
    pairs = expand.shape[1] // 128
    smem = pl.BlockSpec(memory_space=pltpu.SMEM)
    vmem = pl.BlockSpec(memory_space=pltpu.VMEM)
    ext_blocks = blocks + 4 * rims[0].shape[0]
    return pl.pallas_call(
        conv_kernel,
        out_shape=(
            jax.ShapeDtypeStruct((blocks, BLOCK, channels), jnp.float32),
            jax.ShapeDtypeStruct((8, channels), jnp.float32),
        ),
        in_specs=[smem, smem] + [vmem] * 8,
        out_specs=(vmem, vmem),
        scratch_shapes=[
            pltpu.VMEM((ext_blocks, BLOCK, channels), jnp.bfloat16),
            pltpu.VMEM((GROUP * BLOCK, pairs * 256 + channels), jnp.bfloat16),
            pltpu.SMEM((blocks + GROUP,), jnp.int32),
        ],
        compiler_params=pltpu.CompilerParams(vmem_limit_bytes=48 * 1024 * 1024),
    )(sources, used, arrival, *rims, local, expand, weights)


def stats_kernel(nx, ny, population, mine_ref, out_ref, along, every, send1, recv1, send2, recv2):
    tx = lax.axis_index("tx")
    ty = lax.axis_index("ty")
    barrier = pltpu.get_barrier_semaphore()
    for d in range(1, ny):
        pl.semaphore_signal(
            barrier, inc=1, device_id=(tx, lax.rem(ty + d, ny)), device_id_type=MESH
        )
    for d in range(1, nx):
        pl.semaphore_signal(
            barrier, inc=1, device_id=(lax.rem(tx + d, nx), ty), device_id_type=MESH
        )
    pl.semaphore_wait(barrier, nx + ny - 2)

    def first(d):
        return pltpu.make_async_remote_copy(
            src_ref=mine_ref,
            dst_ref=along.at[d],
            send_sem=send1.at[d],
            recv_sem=recv1.at[d],
            device_id=(tx, lax.rem(ty + d, ny)),
            device_id_type=MESH,
        )

    def second(d):
        return pltpu.make_async_remote_copy(
            src_ref=along,
            dst_ref=every.at[d],
            send_sem=send2.at[d],
            recv_sem=recv2.at[d],
            device_id=(lax.rem(tx + d, nx), ty),
            device_id_type=MESH,
        )

    for d in range(1, ny):
        first(d).start()
    along[0] = mine_ref[...]
    for d in range(1, ny):
        first(d).wait_recv()
    for d in range(1, nx):
        second(d).start()
    every[0] = along[...]
    for d in range(1, nx):
        second(d).wait_recv()
    for d in range(1, ny):
        first(d).wait_send()
    for d in range(1, nx):
        second(d).wait_send()
    gathered = every[...]
    total = jnp.sum(gathered[:, :, 0:1, :], axis=(0, 1))
    average = total / population
    away = gathered[:, :, 3:4, :] - average[None, None]
    squares = jnp.sum(
        gathered[:, :, 1:2, :] + gathered[:, :, 2:3, :] * away * away, axis=(0, 1)
    )
    variance = squares / population
    row = lax.broadcasted_iota(jnp.int32, out_ref.shape, 0)
    out_ref[...] = jnp.where(row == 0, average, variance)


def combine(stats, population):
    nx = lax.axis_size("tx")
    ny = lax.axis_size("ty")
    channels = stats.shape[1]
    return pl.pallas_call(
        functools.partial(stats_kernel, nx, ny, population),
        out_shape=jax.ShapeDtypeStruct((8, channels), jnp.float32),
        in_specs=[pl.BlockSpec(memory_space=pltpu.VMEM)],
        out_specs=pl.BlockSpec(memory_space=pltpu.VMEM),
        scratch_shapes=[
            pltpu.VMEM((ny, 8, channels), jnp.float32),
            pltpu.VMEM((nx, ny, 8, channels), jnp.float32),
            pltpu.SemaphoreType.DMA((ny,)),
            pltpu.SemaphoreType.DMA((ny,)),
            pltpu.SemaphoreType.DMA((nx,)),
            pltpu.SemaphoreType.DMA((nx,)),
        ],
        compiler_params=pltpu.CompilerParams(collective_id=1, has_side_effects=True),
    )(stats)


def addresses(target, devices, pair_rows):
    src_count = target.shape[0]
    member = (target[:, None] == jnp.arange(devices, dtype=jnp.int32)[None, :]).astype(jnp.bfloat16)
    run_len = min(512, src_count)
    run_count = src_count // run_len
    member_runs = member.reshape(run_count, run_len, devices)
    lower_ones = (jnp.arange(run_len)[:, None] >= jnp.arange(run_len)[None, :]).astype(jnp.bfloat16)
    inside = jnp.einsum("ij,bjd->bid", lower_ones, member_runs, preferred_element_type=jnp.float32)
    run_totals = inside[:, -1, :]
    before = jnp.cumsum(run_totals, axis=0) - run_totals
    running = (inside + before[:, None, :]).reshape(src_count, devices)
    member_wide = member.astype(jnp.float32)
    placed = jnp.sum((running - 1.0) * member_wide, axis=1).astype(jnp.int32)
    return target * pair_rows + placed


def shards(voxels, owner_tile, rim_blocks, kernel_map, weights, norm_gain, shift_bias):
    devices = lax.axis_size(("tx", "ty"))
    channels = voxels.shape[1]
    tile_rows = kernel_map.shape[2]
    offsets = kernel_map.shape[1]
    middle = offsets // 2
    out_blocks = tile_rows // BLOCK
    pair_rows = tile_rows // devices
    address = addresses(owner_tile[:, 0], devices, pair_rows)
    outgoing = place(address, voxels, tile_rows)
    arrival = lax.all_to_all(
        outgoing.reshape(devices, pair_rows, channels),
        ("tx", "ty"),
        split_axis=0,
        concat_axis=0,
        tiled=True,
    )

    around = jnp.concatenate((kernel_map[0, :middle], kernel_map[0, middle + 1 :]), axis=0)
    around = around.T.reshape(out_blocks, BLOCK, offsets - 1)
    source_block = jnp.maximum(jnp.max(around, axis=1) // BLOCK, 0)
    local = jnp.where(around >= 0, around - source_block[:, None, :] * BLOCK, -1)
    local = jnp.pad(local, ((0, 0), (0, 0), (0, 32 - (offsets - 1))), constant_values=-1)
    local = local.astype(jnp.bfloat16)
    width = (offsets - 1) * BLOCK
    expand = (
        jnp.arange(32, dtype=jnp.int32)[:, None] == jnp.arange(width, dtype=jnp.int32)[None, :] // BLOCK
    ).astype(jnp.bfloat16)
    ordered = jnp.concatenate(
        (weights[:middle], weights[middle + 1 :], weights[middle : middle + 1]), axis=0
    ).reshape(offsets * channels, -1)

    blocked = arrival.reshape(out_blocks, BLOCK, channels)
    used = (blocked[:, 0, 0] >= 0).astype(jnp.int32)
    picked = blocked[rim_blocks[0]]
    rims = (
        from_behind(picked[0], "tx", 1),
        from_behind(picked[1], "tx", -1),
        from_behind(picked[2], "ty", 1),
        from_behind(picked[3], "ty", -1),
    )
    response, stats = convolve(
        source_block.reshape(-1), used, blocked, rims, local, expand, ordered
    )
    population = float(voxels.shape[0] * devices)
    combined = combine(stats, population)
    average, variance = combined[0], combined[1]
    response = response.reshape(tile_rows, channels)
    occupied = (arrival.reshape(tile_rows, channels) >= 0).astype(jnp.float32)
    scaled = norm_gain * (response - average) / jnp.sqrt(variance + 1e-05) + shift_bias
    return (jnp.maximum(scaled, 0.0) * occupied).astype(jnp.bfloat16)


def solution(mesh):
    return jax.shard_map(
        shards,
        mesh=mesh,
        in_specs=(
            P(("tx", "ty"), None),
            P(("tx", "ty"), None),
            P(("tx", "ty"), None, None),
            P(("tx", "ty"), None, None),
            P(),
            P(),
            P(),
        ),
        out_specs=P(("tx", "ty"), None),
        check_vma=False,
    )
```

time: 458 us -> 173 us (0.38)
  matrix products: 175 us -> 0.35 us
  Pallas kernels: 0 us -> 86.9 us
  blocking collectives: 82.5 us -> 0 us
  local copies, waits for them, and re-layouts: 92.9 us -> 12.1 us
  other arithmetic: 30.4 us -> 17.8 us
  loops' own time: 10.7 us -> 0 us
  starting transfers between devices: 19.8 us -> 13.6 us
    dot_general x33 -> x1, matrix products: 175 us -> 0.35 us  [addresses(): jnp.einsum('ij,bjd->bid', lower_ones, member_runs, preferred_element_type...]
    pallas_call x0 -> x3, Pallas kernels: none -> 86.9 us  [the longest x1 44 us: convolve(): pl.pallas_call(conv_kernel, out_shape=(jax.ShapeDtypeStruct((blocks, BLOC...]
    psum x2 -> x0, blocking collectives: 82.5 us -> none  [the longest x1 42.7 us: shards(): average = lax.psum(jnp.sum(response, axis=0), ('tx', 'ty')) / population]
    gather x16 -> x0, local copies, waits for them, and re-layouts: 46 us -> none  [convolve(): fetched = ext_blocks[sources]]
    dynamic_slice x112 -> x0, local copies, waits for them, and re-layouts: 38.5 us -> none  [the longest x96 28.7 us: shards(): lax.map(convolve, (source_groups, local_groups, valid_groups))]
    another operation x2 -> x0, loops' own time: 10.7 us -> none  [the longest x1 10.4 us: shards(): lax.map(place_slots, jnp.arange(tile_rows // slot_len, dtype=jnp.int32))]
    concatenate x2 -> x1, other arithmetic: 7.52 us -> 0.12 us  [shards(): jnp.concatenate((weights[:middle], weights[middle + 1:], weights[middle:m...]
    all_to_all x1 -> x0, starting transfers between devices: 7.3 us -> none  [shards(): lax.all_to_all(filled.reshape(devices, 1), ('tx', 'ty'), split_axis=0, co...]
  transfers between devices with their start and end apart: 6 -> 5, of which waited for: 3 -> 2; matrix products, arithmetic and copies ran while one was open for 16% -> 8% of each run, Pallas kernels for 0% -> 0%
where the time goes in v1:
time: 173 us; the launch traced here: 172 us
  Pallas kernels  86.9 us (50%)
  waiting for transfers between devices  41 us (24%)
  other arithmetic  17.8 us (10%)
  starting transfers between devices  13.6 us (8%)
  local copies, waits for them, and re-layouts  12.1 us (7%)
    pallas_call x1, Pallas kernels, convolve(): pl.pallas_call(conv_kernel, out_shape=(jax.ShapeDtypeStruct((blocks, BLOC...  44 us
    all_to_all x1, waiting for transfers between devices, shards(): lax.all_to_all(outgoing.reshape(devices, pair_rows, channels), ('tx', 'ty...  37 us
    pallas_call x1, Pallas kernels, combine(): pl.pallas_call(functools.partial(stats_kernel, nx, ny, population), out_s...  36.8 us
    all_to_all x1, starting transfers between devices, shards(): lax.all_to_all(outgoing.reshape(devices, pair_rows, channels), ('tx', 'ty...  7.3 us
    ppermute x4, starting transfers between devices, from_behind(): lax.ppermute(value, axis, [(source, source + steps) for source in range(l...  6.32 us
    pallas_call x1, Pallas kernels, place(): pl.pallas_call(place_kernel, out_shape=jax.ShapeDtypeStruct((tile_rows, c...  6.09 us
    convert_element_type x1, other arithmetic, shards(): return (jnp.maximum(scaled, 0.0) * occupied).astype(jnp.bfloat16)  5.03 us
    ppermute x4, waiting for transfers between devices, from_behind(): lax.ppermute(value, axis, [(source, source + steps) for source in range(l...  3.97 us
  transfers between devices with their start and end apart: 5, of which 2 were waited for; matrix products, arithmetic and copies ran while one was open for 8% of the time, Pallas kernels for 0%

profile of v1, /device:TPU:0, one launch (start us, length us, event | category | flops | bytes accessed | tf_op | source)
XLA Modules:
  0.0 172.0 jit_solution(17004695099904943790)
XLA Ops:
  0.0 0.5 broadcast.142
  0.5 1.4 fusion.28
  1.9 0.3 convolution_bitcast_fusion
  2.3 0.2 fusion.29
  2.5 0.2 multiply_reduce_fusion
  2.8 1.2 copy-done.1
  4.0 6.1 %shard_map.73 = bf16[8192,128]{1,0:T(8,128)(2,1)S(1)} custom-call(s32[4096]{0:T(1024)S(1)} %add.60.address_ref, bf16[4096,128]{1,0:T(8,128)(2,1)S(1)} %copy-done.1), custom_call_target="tpu_custom_call" | custom-call | tf_op jit(solution)/shard_map/pallas_call | solution.py:54
  10.1 1.3 copy-done
  11.4 7.3 %all-to-all-start = ((bf16[32,256,128]{2,1,0:T(8,128)(2,1)}), bf16[32,256,128]{2,1,0:T(8,128)(2,1)S(1)}, u32[]{:S(2)}, u32[]{:S(2)}) async-start(bf16[32,256,128]{2,1,0:T(8,128)(2,1)} %bitcast.56), calls=%async_computation | async-start | bytes 4194304 | tf_op jit(solution)/shard_map/all_to_all | solution.py:296
  18.8 0.5 copy_bitcast_fusion
  19.3 0.1 add_bitcast_fusion
  19.4 2.7 %copy.11 = s32[8192,26]{1,0:T(8,128)} copy(s32[8192,26]{0,1:T(8,128)S(1)} %add_bitcast_fusion) | data formatting | bytes 1703936 | tf_op jit(solution)/shard_map/transpose | solution.py:305
  22.2 3.0 %bitcast_reduce_fusion = s32[128,26]{1,0:T(8,128)S(1)} fusion(s32[8192,26]{1,0:T(8,128)} %copy.11), kind=kLoop, calls=%fused_computation.9 | loop fusion | flops 209664 | bytes 865280 | tf_op jit(solution)/shard_map/reduce_max | solution.py:306
  25.2 0.1 reduce_max.12
  25.4 3.0 %fusion.6 = bf16[128,64,26]{2,1,0:T(8,128)(2,1)S(1)} fusion(s32[8192,26]{1,0:T(8,128)} %copy.11, s32[128,26]{1,0:T(8,128)S(1)} %fusion.16), kind=kLoop, calls=%fused_computation.11 | loop fusion | flops 851968 | bytes 1291264 | tf_op jit(solution)/shard_map/convert.1
  28.4 2.0 %pad.5.local_ref = bf16[128,64,32]{2,1,0:T(8,128)(2,1)} pad(bf16[128,64,26]{2,1,0:T(8,128)(2,1)S(1)} %fusion.6, bf16[]{:T(256)} %constant.54.clone.1), padding=0_0x0_0x0_6 | pad | bytes 950274 | tf_op jit(solution)/shard_map/jit(_pad)/pad | solution.py:308
  30.4 0.1 pad_maximum_fusion
  30.6 37.0 %all-to-all-done = bf16[32,256,128]{2,1,0:T(8,128)(2,1)S(1)} async-done(((bf16[32,256,128]{2,1,0:T(8,128)(2,1)}), bf16[32,256,128]{2,1,0:T(8,128)(2,1)S(1)}, u32[]{:S(2)}, u32[]{:S(2)}) %all-to-all-start) | async-done | bytes 2097184 | tf_op jit(solution)/shard_map/all_to_all | solution.py:296
  67.6 2.4 %fusion.17.used_ref = s32[128]{0:T(128)S(1)} fusion(bf16[128,64,128]{2,1,0:T(8,128)(2,1)S(1)} %bitcast.53), kind=kLoop, calls=%fused_computation.37 | loop fusion | flops 256 | bytes 768 | tf_op jit(solution)/shard_map/convert_element_type | solution.py:319
  70.0 1.7 gather_fusion
  71.6 1.3 fusion.25
  72.9 1.4 collective-permute-start
  74.3 1.3 collective-permute-start.1
  75.6 2.3 %collective-permute-start.2 = (bf16[16,64,128]{2,1,0:T(8,128)(2,1)S(1)}, bf16[16,64,128]{2,1,0:T(8,128)(2,1)S(1)}, u32[]{:S(2)}, u32[]{:S(2)}) collective-permute-start(bf16[16,64,128]{2,1,0:T(8,128)(2,1)S(1)} %get-tuple-element.10), channel_id=1, source_target_pairs={{0,1},{1,2},{2,3},{3,4},{4,5},{5,6},{6,7},{8,9},{9,10},{10,11},{11... | collective-permute-start | bytes 786440 | tf_op jit(solution)/shard_map/ppermute | solution.py:17
  78.0 1.3 collective-permute-start.3
  79.2 1.6 broadcast_compare_fusion
  80.8 4.0 %collective-permute-done.1.ux_ref = bf16[16,64,128]{2,1,0:T(8,128)(2,1)S(1)} collective-permute-done((bf16[16,64,128]{2,1,0:T(8,128)(2,1)S(1)}, bf16[16,64,128]{2,1,0:T(8,128)(2,1)S(1)}, u32[]{:S(2)}, u32[]{:S(2)}) %collective-permute-start.1) | collective-permute-done | bytes 262176 | tf_op jit(solution)/shard_map/ppermute | solution.py:17
  84.8 44.0 %shard_map.74 = (f32[128,64,128]{2,1,0:T(8,128)}, f32[8,128]{1,0:T(8,128)S(1)}) custom-call(s32[3328]{0:T(1024)S(1)} %fusion.20.sources_ref, s32[128]{0:T(128)S(1)} %fusion.17.used_ref, bf16[128,64,128]{2,1,0:T(8,128)(2,1)S(1)} %bitcast.55, bf16[16,64,128]{2,1,0:T(8,128)(2,1)S(1)} %collective-permute-done.lx_ref, ...), custom_call_target="tpu_custom_call" | custom-call | tf_op jit(solution)/shard_map/pallas_call | solution.py:172
  128.8 0.6 copy-done.2
  129.4 36.8 %shard_map.75 = f32[8,128]{1,0:T(8,128)} custom-call(f32[8,128]{1,0:T(8,128)} %copy-done.2), custom_call_target="tpu_custom_call" | custom-call | tf_op jit(solution)/shard_map/pallas_call | solution.py:253
  166.2 0.8 slice_bitcast_fusion
  167.0 5.0 %fusion.7 = bf16[8192,128]{1,0:T(8,128)(2,1)} fusion(f32[128,64,128]{2,1,0:T(8,128)} %get-tuple-element.7, pred[32,256,128]{2,1,0:T(8,128)(4,1)} %broadcast_compare_fusion, f32[128]{0:T(128)S(1)} %copy-done.6, f32[128]{0:T(128)S(1)} %get-tuple-element.20, f32[128]{0:T(128)S(1)} %get-tuple-element.19, f32[128]{0:T(128)S(1)} %copy-done.7), kind=kLoop, calls=%fused_computation.12 | loop fusion | flops 7340032 | bytes 7342080 | tf_op jit(solution)/shard_map/convert_element_type | solution.py:336
  (31 shorter events, 0.4 us)
Async XLA Ops:
  1.9 16.8 %copy-start.4 = (s32[1,27,8192]{2,0,1:T(1,128)S(1)}, s32[1,27,8192]{2,0,1:T(1,128)}, u32[]{:S(2)}) copy-start(s32[1,27,8192]{2,0,1:T(1,128)} %param.10) | copy-start | bytes 2654212
  2.8 1.2 copy-start.1
  10.1 1.3 copy-start
  11.4 56.2 %all-to-all-start = ((bf16[32,256,128]{2,1,0:T(8,128)(2,1)}), bf16[32,256,128]{2,1,0:T(8,128)(2,1)S(1)}, u32[]{:S(2)}, u32[]{:S(2)}) async-start(bf16[32,256,128]{2,1,0:T(8,128)(2,1)} %bitcast.56), calls=%async_computation | async-start | bytes 4194304 | tf_op jit(solution)/shard_map/all_to_all | solution.py:296
  18.8 3.3 %copy-start.5 = (s32[1,4,16]{2,1,0:T(4,128)S(1)}, s32[1,4,16]{2,1,0:T(4,128)}, u32[]{:S(2)}) copy-start(s32[1,4,16]{2,1,0:T(4,128)} %param.9) | copy-start | bytes 772
  25.4 5.0 %copy-start.3 = (bf16[27,128,128]{2,1,0:T(8,128)(2,1)S(1)}, bf16[27,128,128]{2,1,0:T(8,128)(2,1)}, u32[]{:S(2)}) copy-start(bf16[27,128,128]{2,1,0:T(8,128)(2,1)} %param.11) | copy-start | bytes 2654212
  28.4 2.1 %slice-start = ((bf16[27,128,128]{2,1,0:T(8,128)(2,1)}), bf16[1,128,128]{2,1,0:T(8,128)(2,1)S(1)}, s32[]{:S(2)}) async-start(bf16[27,128,128]{2,1,0:T(8,128)(2,1)} %param.11), calls=%async_computation.1 | async-start | bytes 65536 | tf_op jit(solution)/shard_map/slice | solution.py:315
  72.9 8.0 %collective-permute-start = (bf16[16,64,128]{2,1,0:T(8,128)(2,1)S(1)}, bf16[16,64,128]{2,1,0:T(8,128)(2,1)S(1)}, u32[]{:S(2)}, u32[]{:S(2)}) collective-permute-start(bf16[16,64,128]{2,1,0:T(8,128)(2,1)S(1)} %get-tuple-element.12), channel_id=1, source_target_pairs={{0,8},{8,16},{16,24},{1,9},{9,17},{17,25},{2,10},{10,18},{18,26},{... | collective-permute-start | bytes 786440 | tf_op jit(solution)/shard_map/ppermute | solution.py:17
  74.3 10.5 %collective-permute-start.1 = (bf16[16,64,128]{2,1,0:T(8,128)(2,1)S(1)}, bf16[16,64,128]{2,1,0:T(8,128)(2,1)S(1)}, u32[]{:S(2)}, u32[]{:S(2)}) collective-permute-start(bf16[16,64,128]{2,1,0:T(8,128)(2,1)S(1)} %get-tuple-element.11), channel_id=1, source_target_pairs={{8,0},{16,8},{24,16},{9,1},{17,9},{25,17},{10,2},{18,10},{26,18},{... | collective-permute-start | bytes 786440 | tf_op jit(solution)/shard_map/ppermute | solution.py:17
  75.6 9.2 %collective-permute-start.2 = (bf16[16,64,128]{2,1,0:T(8,128)(2,1)S(1)}, bf16[16,64,128]{2,1,0:T(8,128)(2,1)S(1)}, u32[]{:S(2)}, u32[]{:S(2)}) collective-permute-start(bf16[16,64,128]{2,1,0:T(8,128)(2,1)S(1)} %get-tuple-element.10), channel_id=1, source_target_pairs={{0,1},{1,2},{2,3},{3,4},{4,5},{5,6},{6,7},{8,9},{9,10},{10,11},{11... | collective-permute-start | bytes 786440 | tf_op jit(solution)/shard_map/ppermute | solution.py:17
  77.9 89.1 %copy-start.6 = (f32[128]{0:T(128)S(1)}, f32[128]{0:T(128)}, u32[]{:S(2)}) copy-start(f32[128]{0:T(128)} %param.13) | copy-start | bytes 1540
  77.9 89.0 %copy-start.7 = (f32[128]{0:T(128)S(1)}, f32[128]{0:T(128)}, u32[]{:S(2)}) copy-start(f32[128]{0:T(128)} %param.12) | copy-start | bytes 1540
  78.0 6.9 %collective-permute-start.3 = (bf16[16,64,128]{2,1,0:T(8,128)(2,1)S(1)}, bf16[16,64,128]{2,1,0:T(8,128)(2,1)S(1)}, u32[]{:S(2)}, u32[]{:S(2)}) collective-permute-start(bf16[16,64,128]{2,1,0:T(8,128)(2,1)S(1)} %get-tuple-element.9), channel_id=1, source_target_pairs={{1,0},{2,1},{3,2},{4,3},{5,4},{6,5},{7,6},{9,8},{10,9},{11,10},{12... | collective-permute-start | bytes 786440 | tf_op jit(solution)/shard_map/ppermute | solution.py:17
  128.8 0.6 copy-start.2

commit v2 on v1

--- a/solution.py
+++ b/solution.py
@@ -9,12 +9,6 @@
 BLOCK = 64
 GROUP = 8
 MESH = pl.DeviceIdType.MESH
-
-
-def from_behind(value, axis, steps):
-    count = lax.axis_size(axis)
-    leading, last = (max(0, -steps), min(count, count - steps))
-    return lax.ppermute(value, axis, [(source, source + steps) for source in range(leading, last)])
 
 
 def place_kernel(address_ref, voxels_ref, out_ref, wide, slots):
@@ -68,13 +62,13 @@
 
 
 def conv_kernel(
-    sources_ref, used_ref, arrival_ref, lx_ref, ux_ref, ly_ref, uy_ref, local_ref, expand_ref,
-    weights_ref, resp_ref, stats_ref, ext, chosen, listed
+    sources_ref, used_ref, arrival_ref, rims_ref, local_ref, expand_ref, weights_ref,
+    resp_ref, stats_ref, ext, chosen, listed
 ):
     blocks = arrival_ref.shape[0]
-    rim = lx_ref.shape[0]
+    rim = rims_ref.shape[0]
     pairs = expand_ref.shape[1] // 128
-    offsets = 2 * pairs
+    middle = pairs
     channels = arrival_ref.shape[2]
     zero16 = jnp.zeros((BLOCK, channels), jnp.bfloat16)
 
@@ -84,12 +78,11 @@
         return carry
 
     def clean_rim(i, carry):
-        for number, ref in enumerate((lx_ref, ux_ref, ly_ref, uy_ref)):
-            ext[blocks + number * rim + i] = jnp.maximum(ref[i], zero16)
+        ext[blocks + i] = jnp.maximum(rims_ref[i], zero16)
         return carry
 
     lax.fori_loop(0, blocks, clean, 0, unroll=4)
-    lax.fori_loop(0, rim, clean_rim, 0)
+    lax.fori_loop(0, rim, clean_rim, 0, unroll=4)
 
     def note(b, count):
         taken = used_ref[b]
@@ -106,13 +99,19 @@
         ids = [listed[w * GROUP + u] for u in range(GROUP)]
         local = jnp.concatenate([local_ref[b] for b in ids], axis=0)
         for p in range(pairs):
-            spread = jnp.dot(
-                local, expand_ref[:, p * 128 : (p + 1) * 128], preferred_element_type=jnp.float32
-            )
-            selector = jnp.where(spread == wanted, 1.0, 0.0).astype(jnp.bfloat16)
+            if p % 2 == 0:
+                width = min(256, (pairs - p) * 128)
+                spread = jnp.dot(
+                    local,
+                    expand_ref[:, p * 128 : p * 128 + width],
+                    preferred_element_type=jnp.float32,
+                )
+            here = spread[:, p % 2 * 128 : p % 2 * 128 + 128]
+            selector = jnp.where(here == wanted, 1.0, 0.0).astype(jnp.bfloat16)
+            k1, k2 = [k + (k >= middle) for k in (2 * p, 2 * p + 1)]
             for u in range(GROUP):
-                first = ext[sources_ref[ids[u] * offsets + 2 * p]]
-                second = ext[sources_ref[ids[u] * offsets + 2 * p + 1]]
+                first = ext[sources_ref[ids[u], k1]]
+                second = ext[sources_ref[ids[u], k2]]
                 both = jnp.concatenate(
                     (
                         jnp.concatenate((first, zero16), axis=1),
@@ -168,14 +167,14 @@
     pairs = expand.shape[1] // 128
     smem = pl.BlockSpec(memory_space=pltpu.SMEM)
     vmem = pl.BlockSpec(memory_space=pltpu.VMEM)
-    ext_blocks = blocks + 4 * rims[0].shape[0]
+    ext_blocks = blocks + rims.shape[0]
     return pl.pallas_call(
         conv_kernel,
         out_shape=(
             jax.ShapeDtypeStruct((blocks, BLOCK, channels), jnp.float32),
             jax.ShapeDtypeStruct((8, channels), jnp.float32),
         ),
-        in_specs=[smem, smem] + [vmem] * 8,
+        in_specs=[smem, smem] + [vmem] * 5,
         out_specs=(vmem, vmem),
         scratch_shapes=[
             pltpu.VMEM((ext_blocks, BLOCK, channels), jnp.bfloat16),
@@ -183,64 +182,60 @@
             pltpu.SMEM((blocks + GROUP,), jnp.int32),
         ],
         compiler_params=pltpu.CompilerParams(vmem_limit_bytes=48 * 1024 * 1024),
-    )(sources, used, arrival, *rims, local, expand, weights)
-
-
-def stats_kernel(nx, ny, population, mine_ref, out_ref, along, every, send1, recv1, send2, recv2):
-    tx = lax.axis_index("tx")
-    ty = lax.axis_index("ty")
+    )(sources, used, arrival, rims, local, expand, weights)
+
+
+def partner(nx, ny, s):
+    tx = lax.rem(lax.axis_index("tx") + lax.rem(s, nx), nx)
+    ty = lax.rem(lax.axis_index("ty") + s // nx, ny)
+    return tx, ty
+
+
+def greet(nx, ny):
     barrier = pltpu.get_barrier_semaphore()
-    for d in range(1, ny):
-        pl.semaphore_signal(
-            barrier, inc=1, device_id=(tx, lax.rem(ty + d, ny)), device_id_type=MESH
-        )
-    for d in range(1, nx):
-        pl.semaphore_signal(
-            barrier, inc=1, device_id=(lax.rem(tx + d, nx), ty), device_id_type=MESH
-        )
-    pl.semaphore_wait(barrier, nx + ny - 2)
-
-    def first(d):
+
+    def call(s, carry):
+        pl.semaphore_signal(barrier, inc=1, device_id=partner(nx, ny, s), device_id_type=MESH)
+        return carry
+
+    lax.fori_loop(1, nx * ny, call, 0)
+    pl.semaphore_wait(barrier, nx * ny - 1)
+
+
+def stats_kernel(nx, ny, population, mine_ref, out_ref, every, send, recv):
+    greet(nx, ny)
+
+    def copy(s):
         return pltpu.make_async_remote_copy(
             src_ref=mine_ref,
-            dst_ref=along.at[d],
-            send_sem=send1.at[d],
-            recv_sem=recv1.at[d],
-            device_id=(tx, lax.rem(ty + d, ny)),
+            dst_ref=every.at[s],
+            send_sem=send.at[s],
+            recv_sem=recv.at[s],
+            device_id=partner(nx, ny, s),
             device_id_type=MESH,
         )
 
-    def second(d):
-        return pltpu.make_async_remote_copy(
-            src_ref=along,
-            dst_ref=every.at[d],
-            send_sem=send2.at[d],
-            recv_sem=recv2.at[d],
-            device_id=(lax.rem(tx + d, nx), ty),
-            device_id_type=MESH,
-        )
-
-    for d in range(1, ny):
-        first(d).start()
-    along[0] = mine_ref[...]
-    for d in range(1, ny):
-        first(d).wait_recv()
-    for d in range(1, nx):
-        second(d).start()
-    every[0] = along[...]
-    for d in range(1, nx):
-        second(d).wait_recv()
-    for d in range(1, ny):
-        first(d).wait_send()
-    for d in range(1, nx):
-        second(d).wait_send()
+    def start(s, carry):
+        copy(s).start()
+        return carry
+
+    def finish(s, carry):
+        copy(s).wait_recv()
+        return carry
+
+    def sent(s, carry):
+        copy(s).wait_send()
+        return carry
+
+    lax.fori_loop(1, nx * ny, start, 0)
+    every[0] = mine_ref[...]
+    lax.fori_loop(1, nx * ny, finish, 0)
+    lax.fori_loop(1, nx * ny, sent, 0)
     gathered = every[...]
-    total = jnp.sum(gathered[:, :, 0:1, :], axis=(0, 1))
+    total = jnp.sum(gathered[:, 0:1, :], axis=0)
     average = total / population
-    away = gathered[:, :, 3:4, :] - average[None, None]
-    squares = jnp.sum(
-        gathered[:, :, 1:2, :] + gathered[:, :, 2:3, :] * away * away, axis=(0, 1)
-    )
+    away = gathered[:, 3:4, :] - average[None]
+    squares = jnp.sum(gathered[:, 1:2, :] + gathered[:, 2:3, :] * away * away, axis=0)
     variance = squares / population
     row = lax.broadcasted_iota(jnp.int32, out_ref.shape, 0)
     out_ref[...] = jnp.where(row == 0, average, variance)
@@ -256,15 +251,144 @@
         in_specs=[pl.BlockSpec(memory_space=pltpu.VMEM)],
         out_specs=pl.BlockSpec(memory_space=pltpu.VMEM),
         scratch_shapes=[
-            pltpu.VMEM((ny, 8, channels), jnp.float32),
-            pltpu.VMEM((nx, ny, 8, channels), jnp.float32),
-            pltpu.SemaphoreType.DMA((ny,)),
-            pltpu.SemaphoreType.DMA((ny,)),
-            pltpu.SemaphoreType.DMA((nx,)),
-            pltpu.SemaphoreType.DMA((nx,)),
+            pltpu.VMEM((nx * ny, 8, channels), jnp.float32),
+            pltpu.SemaphoreType.DMA((nx * ny,)),
+            pltpu.SemaphoreType.DMA((nx * ny,)),
         ],
         compiler_params=pltpu.CompilerParams(collective_id=1, has_side_effects=True),
     )(stats)
+
+
+def exchange_kernel(
+    nx, ny, rim_ref, outgoing_ref, map_ref, arrival_ref, rims_ref, local_ref, sources_ref,
+    staged, send, recv, rim_send, rim_recv
+):
+    tx = lax.axis_index("tx")
+    ty = lax.axis_index("ty")
+    me = tx * ny + ty
+    blocks = arrival_ref.shape[0]
+    per = blocks // (nx * ny)
+    rim = rims_ref.shape[0] // 4
+    greet(nx, ny)
+
+    def copy(s):
+        px, py = partner(nx, ny, s)
+        return pltpu.make_async_remote_copy(
+            src_ref=outgoing_ref.at[pl.ds((px * ny + py) * per, per)],
+            dst_ref=arrival_ref.at[pl.ds(me * per, per)],
+            send_sem=send.at[s],
+            recv_sem=recv.at[s],
+            device_id=(px, py),
+            device_id_type=MESH,
+        )
+
+    def start(s, carry):
+        copy(s).start()
+        return carry
+
+    def finish(s, carry):
+        copy(s).wait_recv()
+        return carry
+
+    def sent(s, carry):
+        copy(s).wait_send()
+        return carry
+
+    lax.fori_loop(1, nx * ny, start, 0)
+    for q in range(per):
+        arrival_ref[me * per + q] = outgoing_ref[me * per + q]
+
+    def prepare(c, carry):
+        turned = map_ref[:, pl.ds(pl.multiple_of(c * 128, 128), 128)].T
+        for h in range(2):
+            rows = turned[h * BLOCK : (h + 1) * BLOCK]
+            source = jnp.maximum(jnp.max(rows, axis=0, keepdims=True), 0) // BLOCK
+            local = jnp.where(rows >= 0, rows - source * BLOCK, -1)
+            local_ref[2 * c + h] = local.astype(jnp.float32).astype(jnp.bfloat16)
+            sources_ref[pl.ds(2 * c + h, 1), :] = source
+        return carry
+
+    lax.fori_loop(0, blocks // 2, prepare, 0)
+    lax.fori_loop(1, nx * ny, finish, 0)
+
+    def stage(i, carry):
+        staged[i] = arrival_ref[rim_ref[i]]
+        return carry
+
+    lax.fori_loop(0, 4 * rim, stage, 0)
+    ways = (
+        (0, (tx + 1, ty), tx < nx - 1, tx > 0),
+        (1, (tx - 1, ty), tx > 0, tx < nx - 1),
+        (2, (tx, ty + 1), ty < ny - 1, ty > 0),
+        (3, (tx, ty - 1), ty > 0, ty < ny - 1),
+    )
+
+    def rim_copy(number, to):
+        return pltpu.make_async_remote_copy(
+            src_ref=staged.at[pl.ds(number * rim, rim)],
+            dst_ref=rims_ref.at[pl.ds(number * rim, rim)],
+            send_sem=rim_send.at[number],
+            recv_sem=rim_recv.at[number],
+            device_id=to,
+            device_id_type=MESH,
+        )
+
+    for number, to, sends, takes in ways:
+
+        @pl.when(sends)
+        def _():
+            rim_copy(number, to).start()
+
+    for number, to, sends, takes in ways:
+
+        @pl.when(jnp.logical_not(takes))
+        def _():
+            rims_ref[pl.ds(number * rim, rim)] = jnp.zeros(
+                (rim,) + rims_ref.shape[1:], jnp.bfloat16
+            )
+
+    for number, to, sends, takes in ways:
+
+        @pl.when(takes)
+        def _():
+            rim_copy(number, to).wait_recv()
+
+        @pl.when(sends)
+        def _():
+            rim_copy(number, to).wait_send()
+
+    lax.fori_loop(1, nx * ny, sent, 0)
+
+
+def exchange(rim_blocks, outgoing, kernel_map):
+    nx = lax.axis_size("tx")
+    ny = lax.axis_size("ty")
+    blocks, _, channels = outgoing.shape
+    rims = rim_blocks.shape[0]
+    wide = kernel_map.shape[0]
+    smem = pl.BlockSpec(memory_space=pltpu.SMEM)
+    vmem = pl.BlockSpec(memory_space=pltpu.VMEM)
+    return pl.pallas_call(
+        functools.partial(exchange_kernel, nx, ny),
+        out_shape=(
+            jax.ShapeDtypeStruct((blocks, BLOCK, channels), jnp.bfloat16),
+            jax.ShapeDtypeStruct((rims, BLOCK, channels), jnp.bfloat16),
+            jax.ShapeDtypeStruct((blocks, BLOCK, wide), jnp.bfloat16),
+            jax.ShapeDtypeStruct((blocks, wide), jnp.int32),
+        ),
+        in_specs=[smem, vmem, vmem],
+        out_specs=(vmem, vmem, vmem, vmem),
+        scratch_shapes=[
+            pltpu.VMEM((rims, BLOCK, channels), jnp.bfloat16),
+            pltpu.SemaphoreType.DMA((nx * ny,)),
+            pltpu.SemaphoreType.DMA((nx * ny,)),
+            pltpu.SemaphoreType.DMA((4,)),
+            pltpu.SemaphoreType.DMA((4,)),
+        ],
+        compiler_params=pltpu.CompilerParams(
+            collective_id=2, has_side_effects=True, vmem_limit_bytes=48 * 1024 * 1024
+        ),
+    )(rim_blocks, outgoing, kernel_map)
 
 
 def addresses(target, devices, pair_rows):
@@ -293,40 +417,18 @@
     pair_rows = tile_rows // devices
     address = addresses(owner_tile[:, 0], devices, pair_rows)
     outgoing = place(address, voxels, tile_rows)
-    arrival = lax.all_to_all(
-        outgoing.reshape(devices, pair_rows, channels),
-        ("tx", "ty"),
-        split_axis=0,
-        concat_axis=0,
-        tiled=True,
+    padded = jnp.pad(kernel_map[0], ((0, 32 - offsets), (0, 0)), constant_values=-1)
+    arrival, rims, local, sources = exchange(
+        rim_blocks.reshape(-1), outgoing.reshape(out_blocks, BLOCK, channels), padded
     )
-
-    around = jnp.concatenate((kernel_map[0, :middle], kernel_map[0, middle + 1 :]), axis=0)
-    around = around.T.reshape(out_blocks, BLOCK, offsets - 1)
-    source_block = jnp.maximum(jnp.max(around, axis=1) // BLOCK, 0)
-    local = jnp.where(around >= 0, around - source_block[:, None, :] * BLOCK, -1)
-    local = jnp.pad(local, ((0, 0), (0, 0), (0, 32 - (offsets - 1))), constant_values=-1)
-    local = local.astype(jnp.bfloat16)
-    width = (offsets - 1) * BLOCK
-    expand = (
-        jnp.arange(32, dtype=jnp.int32)[:, None] == jnp.arange(width, dtype=jnp.int32)[None, :] // BLOCK
-    ).astype(jnp.bfloat16)
+    column = jnp.arange((offsets - 1) * BLOCK, dtype=jnp.int32) // BLOCK
+    column = column + (column >= middle)
+    expand = (jnp.arange(32, dtype=jnp.int32)[:, None] == column[None, :]).astype(jnp.bfloat16)
     ordered = jnp.concatenate(
         (weights[:middle], weights[middle + 1 :], weights[middle : middle + 1]), axis=0
     ).reshape(offsets * channels, -1)
-
-    blocked = arrival.reshape(out_blocks, BLOCK, channels)
-    used = (blocked[:, 0, 0] >= 0).astype(jnp.int32)
-    picked = blocked[rim_blocks[0]]
-    rims = (
-        from_behind(picked[0], "tx", 1),
-        from_behind(picked[1], "tx", -1),
-        from_behind(picked[2], "ty", 1),
-        from_behind(picked[3], "ty", -1),
-    )
-    response, stats = convolve(
-        source_block.reshape(-1), used, blocked, rims, local, expand, ordered
-    )
+    used = (arrival[:, 0, 0] >= 0).astype(jnp.int32)
+    response, stats = convolve(sources, used, arrival, rims, local, expand, ordered)
     population = float(voxels.shape[0] * devices)
     combined = combine(stats, population)
     average, variance = combined[0], combined[1]

time: 173 us -> 169 us (0.977)
  Pallas kernels: 86.9 us -> 153 us
  waiting for transfers between devices: 41 us -> 0 us
  starting transfers between devices: 13.6 us -> 0 us
  other arithmetic: 17.8 us -> 10.4 us
  local copies, waits for them, and re-layouts: 12.1 us -> 5.3 us
    pallas_call x0 -> x1, Pallas kernels: none -> 65 us  [exchange(): pl.pallas_call(functools.partial(exchange_kernel, nx, ny), out_shape=(jax...]
    all_to_all x1 -> x0, waiting for transfers between devices: 37 us -> none  [shards(): lax.all_to_all(outgoing.reshape(devices, pair_rows, channels), ('tx', 'ty...]
    all_to_all x1 -> x0, starting transfers between devices: 7.3 us -> none  [shards(): lax.all_to_all(outgoing.reshape(devices, pair_rows, channels), ('tx', 'ty...]
    ppermute x4 -> x0, starting transfers between devices: 6.32 us -> none  [from_behind(): lax.ppermute(value, axis, [(source, source + steps) for source in range(l...]
    pallas_call x1, Pallas kernels: 36.8 us -> 42.3 us  [combine(): pl.pallas_call(functools.partial(stats_kernel, nx, ny, population), out_s...]
    pallas_call x1, Pallas kernels: 44 us -> 39.4 us  [convolve(): pl.pallas_call(conv_kernel, out_shape=(jax.ShapeDtypeStruct((blocks, BLOC...]
    ppermute x4 -> x0, waiting for transfers between devices: 3.97 us -> none  [from_behind(): lax.ppermute(value, axis, [(source, source + steps) for source in range(l...]
    another operation x1 -> x0, other arithmetic: 2.98 us -> none
  transfers between devices with their start and end apart: 5 -> 0, of which waited for: 2 -> 0; matrix products, arithmetic and copies ran while one was open for 8% -> 0% of each run, Pallas kernels for 0% -> 0%
where the time goes in v2:
time: 169 us
  Pallas kernels  153 us (91%)
  other arithmetic  10.4 us (6%)
  local copies, waits for them, and re-layouts  5.3 us (3%)
    pallas_call x1, Pallas kernels, exchange(): pl.pallas_call(functools.partial(exchange_kernel, nx, ny), out_shape=(jax...  65 us
    pallas_call x1, Pallas kernels, combine(): pl.pallas_call(functools.partial(stats_kernel, nx, ny, population), out_s...  42.3 us
    pallas_call x1, Pallas kernels, convolve(): pl.pallas_call(conv_kernel, out_shape=(jax.ShapeDtypeStruct((blocks, BLOC...  39.4 us
    pallas_call x1, Pallas kernels, place(): pl.pallas_call(place_kernel, out_shape=jax.ShapeDtypeStruct((tile_rows, c...  6.09 us
    convert_element_type x1, other arithmetic, shards(): return (jnp.maximum(scaled, 0.0) * occupied).astype(jnp.bfloat16)  4.73 us

profile of v2, /device:TPU:0, one launch (start us, length us, event | category | flops | bytes accessed | tf_op | source)
XLA Modules:
  0.0 169.0 jit_solution(1827181027795015568)
XLA Ops:
  0.0 0.0 copy-start.3
  0.0 0.8 reshape.62.rim_ref
  0.9 0.5 broadcast.66
  1.4 1.4 fusion.19
  2.8 0.8 slice.25
  3.6 0.3 convolution_bitcast_fusion
  3.9 0.0 copy-start.1
  3.9 0.2 fusion.20
  4.2 0.2 multiply_reduce_fusion
  4.4 1.2 fusion.18
  5.6 0.1 pad_maximum_fusion
  5.7 0.0 copy-done.3
  5.7 0.5 copy.11
  6.3 0.1 pad.4.map_ref
  6.3 0.0 copy-done.1
  6.4 6.1 %shard_map.73 = bf16[8192,128]{1,0:T(8,128)(2,1)S(1)} custom-call(s32[4096]{0:T(1024)S(1)} %add.47.address_ref, bf16[4096,128]{1,0:T(8,128)(2,1)S(1)} %copy-done.1), custom_call_target="tpu_custom_call" | custom-call | tf_op jit(solution)/shard_map/pallas_call | solution.py:48
  12.5 0.0 copy-start
  12.5 1.3 copy-done
  13.8 65.0 %shard_map.74 = (bf16[128,64,128]{2,1,0:T(8,128)(2,1)S(1)}, bf16[64,64,128]{2,1,0:T(8,128)(2,1)S(1)}, bf16[128,64,32]{2,1,0:T(8,128)(2,1)}, s32[128,32]{1,0:T(8,128)S(1)}) custom-call(s32[64]{0:T(128)S(1)} %reshape.62.rim_ref, bf16[128,64,128]{2,1,0:T(8,128)(2,1)} %bitcast.35, s32[32,8192]{1,0:T(8,128)S(1)} %pad.4.map_ref), custom_call_target="tpu_custom_call" | custom-call | tf_op jit(solution)/shard_map/pallas_call | solution.py:371
  78.8 2.4 %fusion.12.used_ref = s32[128]{0:T(128)S(1)} fusion(bf16[128,64,128]{2,1,0:T(8,128)(2,1)S(1)} %get-tuple-element.11.arrival_ref), kind=kLoop, calls=%fused_computation.22 | loop fusion | flops 256 | bytes 768 | tf_op jit(solution)/shard_map/convert_element_type | solution.py:430
  81.2 0.0 copy-start.4
  81.2 0.0 copy-start.5
  81.2 39.4 %shard_map.75 = (f32[128,64,128]{2,1,0:T(8,128)}, f32[8,128]{1,0:T(8,128)S(1)}) custom-call(s32[128,32]{1,0:T(8,128)S(1)} %get-tuple-element.12.sources_ref, s32[128]{0:T(128)S(1)} %fusion.12.used_ref, bf16[128,64,128]{2,1,0:T(8,128)(2,1)S(1)} %get-tuple-element.11.arrival_ref, bf16[64,64,128]{2,1,0:T(8,128)(2,1)S(1)} %get-tuple-element.13.rims_ref, ...), custom_call_target="tpu_custom_call" | custom-call | tf_op jit(solution)/shard_map/pallas_call | solution.py:171
  120.6 0.0 copy-start.2
  120.6 0.5 broadcast_compare_fusion
  121.1 0.0 copy-done.2
  121.2 42.3 %shard_map.76 = f32[8,128]{1,0:T(8,128)} custom-call(f32[8,128]{1,0:T(8,128)} %copy-done.2), custom_call_target="tpu_custom_call" | custom-call | tf_op jit(solution)/shard_map/pallas_call | solution.py:248
  163.5 0.8 slice_bitcast_fusion
  164.2 0.0 copy-done.4
  164.2 0.0 copy-done.5
  164.2 4.7 %fusion.5 = bf16[8192,128]{1,0:T(8,128)(2,1)} fusion(f32[128,64,128]{2,1,0:T(8,128)} %get-tuple-element.15, pred[128,64,128]{2,1,0:T(8,128)(4,1)S(1)} %broadcast_compare_fusion, f32[128]{0:T(128)S(1)} %copy-done.4, f32[128]{0:T(128)S(1)} %get-tuple-element.22, f32[128]{0:T(128)S(1)} %get-tuple-element.21, f32[128]{0:T(128)S(1)} %copy-done.5), kind=kLoop, calls=%fused_computation.6 | loop fusion | flops 7340032 | bytes 7342080 | tf_op jit(solution)/shard_map/convert_element_type | solution.py:438
  (6 shorter events, 0.0 us)
Async XLA Ops:
  0.0 5.7 %copy-start.3 = (s32[1,27,8192]{2,0,1:T(1,128)S(1)}, s32[1,27,8192]{2,0,1:T(1,128)}, u32[]{:S(2)}) copy-start(s32[1,27,8192]{2,0,1:T(1,128)} %param.10) | copy-start | bytes 2654212
  3.9 2.4 %copy-start.1 = (bf16[4096,128]{1,0:T(8,128)(2,1)S(1)}, bf16[4096,128]{1,0:T(8,128)(2,1)}, u32[]{:S(2)}) copy-start(bf16[4096,128]{1,0:T(8,128)(2,1)} %voxels_ref.1) | copy-start | bytes 3145732
  12.5 1.3 copy-start
  81.2 83.1 %copy-start.4 = (f32[128]{0:T(128)S(1)}, f32[128]{0:T(128)}, u32[]{:S(2)}) copy-start(f32[128]{0:T(128)} %param.13) | copy-start | bytes 1540
  81.2 83.1 %copy-start.5 = (f32[128]{0:T(128)S(1)}, f32[128]{0:T(128)}, u32[]{:S(2)}) copy-start(f32[128]{0:T(128)} %param.12) | copy-start | bytes 1540
  120.6 0.6 copy-start.2

commit v3 on v2

--- a/solution.py
+++ b/solution.py
@@ -7,7 +7,6 @@
 from jax.sharding import PartitionSpec as P
 
 BLOCK = 64
-GROUP = 8
 MESH = pl.DeviceIdType.MESH
 
 
@@ -62,78 +61,88 @@
 
 
 def conv_kernel(
-    sources_ref, used_ref, arrival_ref, rims_ref, local_ref, expand_ref, weights_ref,
-    resp_ref, stats_ref, ext, chosen, listed
+    sources_ref, arrival_ref, rims_ref, map_ref, weights_ref, resp_ref, stats_ref, table, turned
 ):
     blocks = arrival_ref.shape[0]
     rim = rims_ref.shape[0]
-    pairs = expand_ref.shape[1] // 128
-    middle = pairs
+    offsets = weights_ref.shape[0]
     channels = arrival_ref.shape[2]
+    middle = offsets // 2
+    others = [k for k in range(offsets) if k != middle]
     zero16 = jnp.zeros((BLOCK, channels), jnp.bfloat16)
-
-    def clean(i, carry):
-        ext[i] = jnp.maximum(arrival_ref[i], zero16)
-        resp_ref[i] = jnp.zeros((BLOCK, channels), jnp.float32)
-        return carry
-
-    def clean_rim(i, carry):
-        ext[blocks + i] = jnp.maximum(rims_ref[i], zero16)
-        return carry
-
-    lax.fori_loop(0, blocks, clean, 0, unroll=4)
-    lax.fori_loop(0, rim, clean_rim, 0, unroll=4)
-
-    def note(b, count):
-        taken = used_ref[b]
-        listed[count] = b
-        return count + taken
-
-    count = lax.fori_loop(0, blocks, note, jnp.int32(0))
-    for u in range(GROUP):
-        listed[count + u] = listed[jnp.maximum(count - 1, 0)]
-    lane = lax.broadcasted_iota(jnp.int32, (1, 128), 1)
-    wanted = (lane % BLOCK).astype(jnp.float32)
+    lane = lax.broadcasted_iota(jnp.int32, (channels, 128), 1)
+    left = lane < BLOCK
+    diagonal = lax.broadcasted_iota(jnp.int32, (channels, channels), 0) == (
+        lax.broadcasted_iota(jnp.int32, (channels, channels), 1)
+    )
+    unit = jnp.where(diagonal, 1.0, 0.0).astype(jnp.bfloat16)
+
+    def flip(value):
+        return lax.dot_general(
+            unit, value, (((1,), (1,)), ((), ())), preferred_element_type=jnp.float32
+        )
+
+    def fill(ref, start):
+        def step(i, carry):
+            one = jnp.maximum(ref[2 * i], zero16)
+            two = jnp.maximum(ref[2 * i + 1], zero16)
+            both = flip(jnp.concatenate((one, one, two, two), axis=0))
+            table[start + 2 * i] = both[:, :128]
+            table[start + 2 * i + 1] = both[:, 128:]
+            return carry
+
+        lax.fori_loop(0, ref.shape[0] // 2, step, 0, unroll=4)
+
+    fill(arrival_ref, 0)
+    fill(rims_ref, blocks)
+    for place, k in enumerate(others + [middle]):
+        turned[:, place * channels : (place + 1) * channels] = flip(weights_ref[k]).astype(
+            jnp.bfloat16
+        )
 
     def window(w, carry):
-        ids = [listed[w * GROUP + u] for u in range(GROUP)]
-        local = jnp.concatenate([local_ref[b] for b in ids], axis=0)
-        for p in range(pairs):
-            if p % 2 == 0:
-                width = min(256, (pairs - p) * 128)
-                spread = jnp.dot(
-                    local,
-                    expand_ref[:, p * 128 : p * 128 + width],
-                    preferred_element_type=jnp.float32,
-                )
-            here = spread[:, p % 2 * 128 : p % 2 * 128 + 128]
-            selector = jnp.where(here == wanted, 1.0, 0.0).astype(jnp.bfloat16)
-            k1, k2 = [k + (k >= middle) for k in (2 * p, 2 * p + 1)]
-            for u in range(GROUP):
-                first = ext[sources_ref[ids[u], k1]]
-                second = ext[sources_ref[ids[u], k2]]
-                both = jnp.concatenate(
-                    (
-                        jnp.concatenate((first, zero16), axis=1),
-                        jnp.concatenate((zero16, second), axis=1),
-                    ),
-                    axis=0,
-                )
-                picked = jnp.dot(
-                    selector[u * BLOCK : (u + 1) * BLOCK], both, preferred_element_type=jnp.float32
-                )
-                chosen[u * BLOCK : (u + 1) * BLOCK, p * 256 : (p + 1) * 256] = picked.astype(
-                    jnp.bfloat16
-                )
-        for u in range(GROUP):
-            chosen[u * BLOCK : (u + 1) * BLOCK, pairs * 256 :] = ext[ids[u]]
-        result = jnp.dot(chosen[...], weights_ref[...], preferred_element_type=jnp.float32)
-        for u in range(GROUP):
-            full = arrival_ref[ids[u]].astype(jnp.float32) >= 0.0
-            resp_ref[ids[u]] = jnp.where(full, result[u * BLOCK : (u + 1) * BLOCK], 0.0)
-        return carry
-
-    lax.fori_loop(0, (count + GROUP - 1) // GROUP, window, 0)
+        def pick(k, c):
+            b = 2 * (2 * w + c)
+            at = pl.ds(pl.multiple_of((2 * w + c) * 128, 128), 128)
+            entry = map_ref[k : k + 1, at]
+            spot = lax.rem(jnp.maximum(entry, 0), BLOCK) + jnp.where(left[:1], 0, BLOCK)
+            spot = jnp.broadcast_to(spot, (channels, 128))
+            source = jnp.where(left, table[sources_ref[b, k]], table[sources_ref[b + 1, k]])
+            found = jnp.take_along_axis(source, spot, axis=1)
+            return jnp.where(entry >= 0, found, 0.0).astype(jnp.bfloat16)
+
+        def straight(c):
+            b = 2 * (2 * w + c)
+            return jnp.where(left, table[b], table[b + 1]).astype(jnp.bfloat16)
+
+        result = jnp.dot(
+            turned[:, (offsets - 1) * channels :],
+            jnp.concatenate((straight(0), straight(1)), axis=1),
+            preferred_element_type=jnp.float32,
+        )
+        for p in range(len(others) // 2):
+            k1, k2 = others[2 * p : 2 * p + 2]
+            chosen = jnp.concatenate(
+                (
+                    jnp.concatenate((pick(k1, 0), pick(k1, 1)), axis=1),
+                    jnp.concatenate((pick(k2, 0), pick(k2, 1)), axis=1),
+                ),
+                axis=0,
+            )
+            result += jnp.dot(
+                turned[:, 2 * p * channels : (2 * p + 2) * channels],
+                chosen,
+                preferred_element_type=jnp.float32,
+            )
+        for c in range(2):
+            rows = result[:, c * 128 : (c + 1) * 128].T
+            for h in range(2):
+                b = 4 * w + 2 * c + h
+                full = arrival_ref[b].astype(jnp.float32) >= 0.0
+                resp_ref[b] = jnp.where(full, rows[h * BLOCK : (h + 1) * BLOCK], 0.0)
+        return carry
+
+    lax.fori_loop(0, blocks // 4, window, 0)
 
     def add(i, carry):
         total, number = carry
@@ -162,9 +171,9 @@
     )
 
 
-def convolve(sources, used, arrival, rims, local, expand, weights):
+def convolve(sources, arrival, rims, kernel_map, weights):
     blocks, _, channels = arrival.shape
-    pairs = expand.shape[1] // 128
+    offsets = weights.shape[0]
     smem = pl.BlockSpec(memory_space=pltpu.SMEM)
     vmem = pl.BlockSpec(memory_space=pltpu.VMEM)
     ext_blocks = blocks + rims.shape[0]
@@ -174,15 +183,14 @@
             jax.ShapeDtypeStruct((blocks, BLOCK, channels), jnp.float32),
             jax.ShapeDtypeStruct((8, channels), jnp.float32),
         ),
-        in_specs=[smem, smem] + [vmem] * 5,
+        in_specs=[smem] + [vmem] * 4,
         out_specs=(vmem, vmem),
         scratch_shapes=[
-            pltpu.VMEM((ext_blocks, BLOCK, channels), jnp.bfloat16),
-            pltpu.VMEM((GROUP * BLOCK, pairs * 256 + channels), jnp.bfloat16),
-            pltpu.SMEM((blocks + GROUP,), jnp.int32),
+            pltpu.VMEM((ext_blocks, channels, 128), jnp.float32),
+            pltpu.VMEM((channels, offsets * channels), jnp.bfloat16),
         ],
         compiler_params=pltpu.CompilerParams(vmem_limit_bytes=48 * 1024 * 1024),
-    )(sources, used, arrival, rims, local, expand, weights)
+    )(sources, arrival, rims, kernel_map, weights)
 
 
 def partner(nx, ny, s):
@@ -260,7 +268,7 @@
 
 
 def exchange_kernel(
-    nx, ny, rim_ref, outgoing_ref, map_ref, arrival_ref, rims_ref, local_ref, sources_ref,
+    nx, ny, rim_ref, outgoing_ref, map_ref, arrival_ref, rims_ref, sources_ref,
     staged, send, recv, rim_send, rim_recv
 ):
     tx = lax.axis_index("tx")
@@ -303,8 +311,6 @@
         for h in range(2):
             rows = turned[h * BLOCK : (h + 1) * BLOCK]
             source = jnp.maximum(jnp.max(rows, axis=0, keepdims=True), 0) // BLOCK
-            local = jnp.where(rows >= 0, rows - source * BLOCK, -1)
-            local_ref[2 * c + h] = local.astype(jnp.float32).astype(jnp.bfloat16)
             sources_ref[pl.ds(2 * c + h, 1), :] = source
         return carry
 
@@ -373,11 +379,10 @@
         out_shape=(
             jax.ShapeDtypeStruct((blocks, BLOCK, channels), jnp.bfloat16),
             jax.ShapeDtypeStruct((rims, BLOCK, channels), jnp.bfloat16),
-            jax.ShapeDtypeStruct((blocks, BLOCK, wide), jnp.bfloat16),
             jax.ShapeDtypeStruct((blocks, wide), jnp.int32),
         ),
         in_specs=[smem, vmem, vmem],
-        out_specs=(vmem, vmem, vmem, vmem),
+        out_specs=(vmem, vmem, vmem),
         scratch_shapes=[
             pltpu.VMEM((rims, BLOCK, channels), jnp.bfloat16),
             pltpu.SemaphoreType.DMA((nx * ny,)),
@@ -412,23 +417,15 @@
     channels = voxels.shape[1]
     tile_rows = kernel_map.shape[2]
     offsets = kernel_map.shape[1]
-    middle = offsets // 2
     out_blocks = tile_rows // BLOCK
     pair_rows = tile_rows // devices
     address = addresses(owner_tile[:, 0], devices, pair_rows)
     outgoing = place(address, voxels, tile_rows)
     padded = jnp.pad(kernel_map[0], ((0, 32 - offsets), (0, 0)), constant_values=-1)
-    arrival, rims, local, sources = exchange(
+    arrival, rims, sources = exchange(
         rim_blocks.reshape(-1), outgoing.reshape(out_blocks, BLOCK, channels), padded
     )
-    column = jnp.arange((offsets - 1) * BLOCK, dtype=jnp.int32) // BLOCK
-    column = column + (column >= middle)
-    expand = (jnp.arange(32, dtype=jnp.int32)[:, None] == column[None, :]).astype(jnp.bfloat16)
-    ordered = jnp.concatenate(
-        (weights[:middle], weights[middle + 1 :], weights[middle : middle + 1]), axis=0
-    ).reshape(offsets * channels, -1)
-    used = (arrival[:, 0, 0] >= 0).astype(jnp.int32)
-    response, stats = convolve(sources, used, arrival, rims, local, expand, ordered)
+    response, stats = convolve(sources, arrival, rims, padded, weights)
     population = float(voxels.shape[0] * devices)
     combined = combine(stats, population)
     average, variance = combined[0], combined[1]

time: 169 us -> 139 us (0.82)
  Pallas kernels: 153 us -> 125 us
  other arithmetic: 10.4 us -> 7.85 us
    pallas_call x1, Pallas kernels: 42.3 us -> 11.1 us  [combine(): pl.pallas_call(functools.partial(stats_kernel, nx, ny, population), out_s...]
    pallas_call x1, Pallas kernels: 39.4 us -> 43.8 us  [convolve(): pl.pallas_call(conv_kernel, out_shape=(jax.ShapeDtypeStruct((blocks, BLOC...]
    unnamed x15 -> x19, local copies, waits for them, and re-layouts: 2.42 us -> 5.36 us
    convert_element_type x2 -> x0, other arithmetic: 2.38 us -> none  [the longest x1 2.36 us: shards(): used = (arrival[:, 0, 0] >= 0).astype(jnp.int32)]
    slice x2 -> x0, local copies, waits for them, and re-layouts: 1.96 us -> none  [the longest x1 1.19 us: shards(): weights[:middle]]
where the time goes in v3:
time: 139 us
  Pallas kernels  125 us (90%)
  other arithmetic  7.85 us (6%)
  local copies, waits for them, and re-layouts  5.52 us (4%)
    pallas_call x1, Pallas kernels, exchange(): pl.pallas_call(functools.partial(exchange_kernel, nx, ny), out_shape=(jax...  63.7 us
    pallas_call x1, Pallas kernels, convolve(): pl.pallas_call(conv_kernel, out_shape=(jax.ShapeDtypeStruct((blocks, BLOC...  43.8 us
    pallas_call x1, Pallas kernels, combine(): pl.pallas_call(functools.partial(stats_kernel, nx, ny, population), out_s...  11.1 us
    pallas_call x1, Pallas kernels, place(): pl.pallas_call(place_kernel, out_shape=jax.ShapeDtypeStruct((tile_rows, c...  6.09 us
    unnamed x19, local copies, waits for them, and re-layouts  5.36 us
    convert_element_type x1, other arithmetic, shards(): return (jnp.maximum(scaled, 0.0) * occupied).astype(jnp.bfloat16)  4.73 us

profile of v3, /device:TPU:0, one launch (start us, length us, event | category | flops | bytes accessed | tf_op | source)
XLA Modules:
  0.0 138.6 jit_solution(15415610176085380538)
XLA Ops:
  0.0 0.0 copy-start.4
  0.0 0.5 broadcast.30
  0.5 1.4 %fusion.11 = (s32[4096]{0:T(1024)S(1)}, s32[4096,1]{0,1:T(1,128)S(1)}) fusion(s32[4096,1]{0,1:T(1,128)} %param.8, s32[]{:T(128)} %broadcast.30), kind=kLoop, calls=%fused_computation.22 | loop fusion | flops 4096 | bytes 49156 | tf_op args[1]
  1.9 0.0 copy-start.5
  1.9 0.3 convolution_bitcast_fusion
  2.3 0.2 fusion.12
  2.5 0.2 multiply_reduce_fusion
  2.8 0.0 copy-start.1
  2.8 1.2 copy-done.1
  4.0 6.1 %shard_map.73 = bf16[8192,128]{1,0:T(8,128)(2,1)S(1)} custom-call(s32[4096]{0:T(1024)S(1)} %add.35.address_ref, bf16[4096,128]{1,0:T(8,128)(2,1)S(1)} %copy-done.1), custom_call_target="tpu_custom_call" | custom-call | tf_op jit(solution)/shard_map/pallas_call | solution.py:47
  10.1 0.0 copy-start
  10.1 1.3 copy-done
  11.4 0.0 copy-done.4
  11.4 0.5 copy.11
  11.9 0.1 pad.4.map_ref
  12.0 0.0 copy-done.5
  12.0 0.1 reshape.39.rim_ref
  12.1 63.7 %shard_map.74 = (bf16[128,64,128]{2,1,0:T(8,128)(2,1)S(1)}, bf16[64,64,128]{2,1,0:T(8,128)(2,1)S(1)}, s32[128,32]{1,0:T(8,128)S(1)}) custom-call(s32[64]{0:T(128)S(1)} %reshape.39.rim_ref, bf16[128,64,128]{2,1,0:T(8,128)(2,1)} %bitcast.34, s32[32,8192]{1,0:T(8,128)S(1)} %pad.4.map_ref), custom_call_target="tpu_custom_call" | custom-call | tf_op jit(solution)/shard_map/pallas_call | solution.py:377
  75.8 0.0 copy-start.6
  75.8 0.0 copy-start.7
  75.8 0.0 copy-start.2
  75.8 1.2 copy-done.2
  77.0 43.8 %shard_map.75 = (f32[128,64,128]{2,1,0:T(8,128)}, f32[8,128]{1,0:T(8,128)S(1)}) custom-call(s32[128,32]{1,0:T(8,128)S(1)} %get-tuple-element.11.sources_ref, bf16[128,64,128]{2,1,0:T(8,128)(2,1)S(1)} %get-tuple-element.10.arrival_ref, bf16[64,64,128]{2,1,0:T(8,128)(2,1)S(1)} %get-tuple-element.12.rims_ref, s32[32,8192]{1,0:T(8,128)S(1)} %pad.4.map_ref, ...), custom_call_target="tpu_custom_call" | custom-call | tf_op jit(solution)/shard_map/pallas_call | solution.py:180
  120.8 0.0 copy-start.3
  120.8 0.6 copy-done.3
  121.4 11.1 %shard_map.76 = f32[8,128]{1,0:T(8,128)} custom-call(f32[8,128]{1,0:T(8,128)} %copy-done.3), custom_call_target="tpu_custom_call" | custom-call | tf_op jit(solution)/shard_map/pallas_call | solution.py:256
  132.5 0.8 slice_bitcast_fusion
  133.3 0.5 broadcast_compare_fusion
  133.8 0.0 copy-done.6
  133.9 0.0 copy-done.7
  133.9 4.7 %fusion.5 = bf16[8192,128]{1,0:T(8,128)(2,1)} fusion(f32[128,64,128]{2,1,0:T(8,128)} %get-tuple-element.13, pred[128,64,128]{2,1,0:T(8,128)(4,1)S(1)} %broadcast_compare_fusion, f32[128]{0:T(128)S(1)} %copy-done.6, f32[128]{0:T(128)S(1)} %get-tuple-element.18, f32[128]{0:T(128)S(1)} %get-tuple-element.17, f32[128]{0:T(128)S(1)} %copy-done.7), kind=kLoop, calls=%fused_computation.6 | loop fusion | flops 7340032 | bytes 7342080 | tf_op jit(solution)/shard_map/convert_element_type | solution.py:435
  (4 shorter events, 0.0 us)
Async XLA Ops:
  0.0 11.4 %copy-start.4 = (s32[1,27,8192]{2,0,1:T(1,128)S(1)}, s32[1,27,8192]{2,0,1:T(1,128)}, u32[]{:S(2)}) copy-start(s32[1,27,8192]{2,0,1:T(1,128)} %param.10) | copy-start | bytes 2654212
  1.9 10.1 %copy-start.5 = (s32[1,4,16]{2,1,0:T(4,128)S(1)}, s32[1,4,16]{2,1,0:T(4,128)}, u32[]{:S(2)}) copy-start(s32[1,4,16]{2,1,0:T(4,128)} %param.9) | copy-start | bytes 772
  2.8 1.2 copy-start.1
  10.1 1.3 copy-start
  75.8 58.1 %copy-start.6 = (f32[128]{0:T(128)S(1)}, f32[128]{0:T(128)}, u32[]{:S(2)}) copy-start(f32[128]{0:T(128)} %param.13) | copy-start | bytes 1540
  75.8 58.1 %copy-start.7 = (f32[128]{0:T(128)S(1)}, f32[128]{0:T(128)}, u32[]{:S(2)}) copy-start(f32[128]{0:T(128)} %param.12) | copy-start | bytes 1540
  75.8 1.2 copy-start.2
  120.8 0.6 copy-start.3

commit v4 on v0

v4 whole, which is shorter than its diff:
```python
import functools
import jax
import jax.numpy as jnp
from jax import lax
from jax.experimental import pallas as pl
from jax.experimental.pallas import tpu as pltpu
from jax.sharding import PartitionSpec as P

BLOCK = 64
MESH = pl.DeviceIdType.MESH


def place_kernel(address_ref, voxels_ref, out_ref, wide, slots):
    rows = voxels_ref.shape[0]
    total = slots.shape[0]
    chunk = 256

    def widen(i, carry):
        at = pl.ds(pl.multiple_of(i * chunk, chunk), chunk)
        wide[at, :] = voxels_ref[at, :].astype(jnp.float32)
        return carry

    def clear(i, carry):
        at = pl.ds(pl.multiple_of(i * chunk, chunk), chunk)
        slots[at, :] = jnp.full((chunk, slots.shape[1]), -1.0, jnp.float32)
        return carry

    def put(i, carry):
        base = pl.multiple_of(i * 16, 16)
        for u in range(16):
            slots[pl.ds(address_ref[base + u], 1), :] = wide[pl.ds(base + u, 1), :]
        return carry

    left = lax.broadcasted_iota(jnp.int32, (BLOCK // 2, slots.shape[1]), 1) < slots.shape[1] // 2

    def narrow(b, carry):
        block = slots[pl.ds(pl.multiple_of(b * BLOCK, BLOCK), BLOCK), :]
        upper, lower = block[: BLOCK // 2], block[BLOCK // 2 :]
        half = slots.shape[1] // 2
        out_ref[0, b] = jnp.where(left, upper, pltpu.roll(lower, half, 1)).astype(jnp.bfloat16)
        out_ref[1, b] = jnp.where(left, pltpu.roll(upper, half, 1), lower).astype(jnp.bfloat16)
        return carry

    lax.fori_loop(0, rows // chunk, widen, 0)
    lax.fori_loop(0, total // chunk, clear, 0)
    lax.fori_loop(0, rows // 16, put, 0)
    lax.fori_loop(0, total // BLOCK, narrow, 0, unroll=4)


def place(address, voxels, tile_rows):
    rows, channels = voxels.shape
    return pl.pallas_call(
        place_kernel,
        out_shape=jax.ShapeDtypeStruct(
            (2, tile_rows // BLOCK, BLOCK // 2, channels), jnp.bfloat16
        ),
        in_specs=[
            pl.BlockSpec(memory_space=pltpu.SMEM),
            pl.BlockSpec(memory_space=pltpu.VMEM),
        ],
        out_specs=pl.BlockSpec(memory_space=pltpu.VMEM),
        scratch_shapes=[
            pltpu.VMEM((rows, channels), jnp.float32),
            pltpu.VMEM((tile_rows, channels), jnp.float32),
        ],
        compiler_params=pltpu.CompilerParams(vmem_limit_bytes=32 * 1024 * 1024),
    )(address, voxels)


def partner(nx, ny, s):
    tx = lax.rem(lax.axis_index("tx") + lax.rem(s, nx), nx)
    ty = lax.rem(lax.axis_index("ty") + s // nx, ny)
    return tx, ty


def layer_kernel(
    nx, ny, population, rim_ref, outgoing_ref, map_ref, weights_ref, resp_ref, out_ref,
    arrival0, arrival1, staged, rims, found_v, found_s, table, turned, partial, filled, mine, every,
    send, recv, rim_send, rim_recv, stat_send, stat_recv, local_sem
):
    tx = lax.axis_index("tx")
    ty = lax.axis_index("ty")
    me = tx * ny + ty
    count = nx * ny
    arrival = (arrival0, arrival1)
    blocks = arrival0.shape[0]
    per = blocks // count
    rim = rims.shape[1] // 4
    offsets = weights_ref.shape[0]
    channels = weights_ref.shape[1]
    half = channels // 2
    middle = offsets // 2
    order = [k for k in range(offsets) if k != middle] + [middle]

    barrier = pltpu.get_barrier_semaphore()

    def call(s, carry):
        pl.semaphore_signal(barrier, inc=1, device_id=partner(nx, ny, s), device_id_type=MESH)
        return carry

    lax.fori_loop(1, count, call, 0)
    pl.semaphore_wait(barrier, count - 1)

    def copy(h, s):
        px, py = partner(nx, ny, s)
        return pltpu.make_async_remote_copy(
            src_ref=outgoing_ref.at[h, pl.ds((px * ny + py) * per, per)],
            dst_ref=arrival[h].at[pl.ds(me * per, per)],
            send_sem=send.at[h, s],
            recv_sem=recv.at[h, s],
            device_id=(px, py),
            device_id_type=MESH,
        )

    def each(act):
        def step(s, carry):
            act(s)
            return carry

        lax.fori_loop(1, count, step, 0)

    ways = (
        (0, (tx + 1, ty), tx < nx - 1, tx > 0),
        (1, (tx - 1, ty), tx > 0, tx < nx - 1),
        (2, (tx, ty + 1), ty < ny - 1, ty > 0),
        (3, (tx, ty - 1), ty > 0, ty < ny - 1),
    )

    def rim_copy(h, number, to):
        return pltpu.make_async_remote_copy(
            src_ref=staged.at[h, pl.ds(number * rim, rim)],
            dst_ref=rims.at[h, pl.ds(number * rim, rim)],
            send_sem=rim_send.at[h, number],
            recv_sem=rim_recv.at[h, number],
            device_id=to,
            device_id_type=MESH,
        )

    def send_rims(h):
        def stage(i, carry):
            staged[h, i] = arrival[h][rim_ref[i]]
            return carry

        lax.fori_loop(0, 4 * rim, stage, 0)
        for number, to, sends, takes in ways:

            @pl.when(sends)
            def _():
                rim_copy(h, number, to).start()

            @pl.when(jnp.logical_not(takes))
            def _():
                rims[h, pl.ds(number * rim, rim)] = jnp.zeros((rim,) + rims.shape[2:], jnp.bfloat16)

    def take_rims(h):
        for number, to, sends, takes in ways:

            @pl.when(takes)
            def _():
                rim_copy(h, number, to).wait_recv()

    def drain(h):
        each(lambda s: copy(h, s).wait_send())
        for number, to, sends, takes in ways:

            @pl.when(sends)
            def _():
                rim_copy(h, number, to).wait_send()

    each(lambda s: copy(0, s).start())
    for h in range(2):
        for q in range(per):
            arrival[h][me * per + q] = outgoing_ref[h, me * per + q]

    found_v[...] = jnp.zeros_like(found_v)

    def prepare(c, carry):
        columns = map_ref[:, pl.ds(pl.multiple_of(c * 128, 128), 128)].T
        for i in range(2):
            rows = columns[i * BLOCK : (i + 1) * BLOCK]
            source = jnp.maximum(jnp.max(rows, axis=0, keepdims=True), 0) // BLOCK
            found_v[pl.ds(2 * c + i, 1), 0 : map_ref.shape[0]] = source
        return carry

    lax.fori_loop(0, blocks // 2, prepare, 0)
    inward = pltpu.make_async_copy(found_v, found_s, local_sem)
    inward.start()

    row_at = lax.broadcasted_iota(jnp.int32, (channels, channels), 0)
    lane_at = lax.broadcasted_iota(jnp.int32, (channels, channels), 1)
    unit = jnp.where(row_at == lane_at, 1.0, 0.0).astype(jnp.bfloat16)
    top_at = lax.broadcasted_iota(jnp.int32, (half, 2 * channels), 0)
    wide_at = lax.broadcasted_iota(jnp.int32, (half, 2 * channels), 1)
    halves = (wide_at == top_at) | (wide_at == top_at + channels + half)
    halves = jnp.where(halves, 1.0, 0.0).astype(jnp.bfloat16)
    left = lane_at[:half] < BLOCK

    def flip(value, by):
        return lax.dot_general(
            by, value, (((1,), (1,)), ((), ())), preferred_element_type=jnp.float32
        )

    nothing16 = jnp.zeros((half, channels), jnp.bfloat16)
    for h in range(2):
        for p in range((offsets + 1) // 2):
            one = weights_ref[order[2 * p]][h * half : (h + 1) * half]
            two = nothing16
            if 2 * p + 1 < offsets:
                two = weights_ref[order[2 * p + 1]][h * half : (h + 1) * half]
            turned[h, :, p * channels : (p + 1) * channels] = flip(
                jnp.concatenate((one, two), axis=0), unit
            ).astype(jnp.bfloat16)
    inward.wait()

    quiet = jnp.zeros((BLOCK // 2, channels), jnp.bfloat16)

    def block_table(block):
        first = jnp.concatenate((block, quiet, block, quiet), axis=0)
        second = jnp.concatenate((quiet, block, quiet, block), axis=0)
        return flip(jnp.concatenate((first, second), axis=1), halves)

    def fill_tile(h):
        def step(c, carry):
            one = block_table(arrival[h][2 * c])
            two = block_table(arrival[h][2 * c + 1])
            table[2 * c] = jnp.maximum(one, 0.0)
            table[2 * c + 1] = jnp.maximum(two, 0.0)
            if h == 1:
                filled[c] = jnp.where(left[:8], one[:8], two[:8])
            return carry

        lax.fori_loop(0, blocks // 2, step, 0, unroll=4)

    def fill_rims(h):
        def step(i, carry):
            table[blocks + i] = jnp.maximum(block_table(rims[h, i]), 0.0)
            return carry

        lax.fori_loop(0, 4 * rim, step, 0, unroll=4)

    marker = -1e30

    def convolve(h):
        def window(w, carry):
            def pick(k, c):
                b = 2 * (2 * w + c)
                if k == middle:
                    return jnp.where(left, table[b], table[b + 1]).astype(jnp.bfloat16)
                at = pl.ds(pl.multiple_of((2 * w + c) * 128, 128), 128)
                entry = map_ref[k : k + 1, at]
                spot = lax.rem(jnp.maximum(entry, 0), BLOCK) + jnp.where(left[:1], 0, BLOCK)
                spot = jnp.broadcast_to(spot, (half, 128))
                source = jnp.where(left, table[found_s[b, k]], table[found_s[b + 1, k]])
                taken = jnp.take_along_axis(source, spot, axis=1)
                return jnp.where(entry >= 0, taken, 0.0).astype(jnp.bfloat16)

            result = None
            for p in range((offsets + 3) // 4):
                parts = [
                    jnp.concatenate((pick(k, 0), pick(k, 1)), axis=1)
                    for k in order[4 * p : 4 * p + 4]
                ]
                while len(parts) % 2:
                    parts.append(jnp.zeros((half, 256), jnp.bfloat16))
                depth = len(parts) * half
                term = jnp.dot(
                    turned[h, :, p * 4 * half : p * 4 * half + depth],
                    jnp.concatenate(parts, axis=0),
                    preferred_element_type=jnp.float32,
                )
                result = term if result is None else result + term
            if h == 0:
                partial[w] = result
            else:
                result = result + partial[w]
                for c in range(2):
                    here = filled[2 * w + c][0:1] >= 0.0
                    rows = jnp.where(here, result[:, c * 128 : (c + 1) * 128], marker).T
                    resp_ref[pl.ds(pl.multiple_of((2 * w + c) * 128, 128), 128), :] = rows
            return carry

        lax.fori_loop(0, blocks // 4, window, 0)

    each(lambda s: copy(0, s).wait_recv())
    send_rims(0)
    each(lambda s: copy(1, s).start())
    fill_tile(0)
    take_rims(0)
    fill_rims(0)
    convolve(0)
    each(lambda s: copy(1, s).wait_recv())
    send_rims(1)
    fill_tile(1)
    take_rims(1)
    fill_rims(1)
    convolve(1)

    def rows_of(i):
        value = resp_ref[pl.ds(pl.multiple_of(i * BLOCK, BLOCK), BLOCK), :]
        return value, value > marker * 0.5

    def fold(value):
        return jnp.sum(value.reshape(BLOCK // 8, 8, channels), axis=0)

    def add(i, carry):
        value, full = rows_of(i)
        return (
            carry[0] + fold(jnp.where(full, value, 0.0)),
            carry[1] + fold(jnp.where(full, 1.0, 0.0)),
        )

    nothing = jnp.zeros((8, channels), jnp.float32)
    total, number = lax.fori_loop(0, blocks, add, (nothing, nothing), unroll=4)
    total = jnp.sum(total, axis=0, keepdims=True)
    number = jnp.sum(number, axis=0, keepdims=True)
    mean = total / jnp.maximum(number, 1.0)

    def spread_of(i, squares):
        value, full = rows_of(i)
        off = jnp.where(full, value - mean, 0.0)
        return squares + fold(off * off)

    squares = lax.fori_loop(0, blocks, spread_of, nothing, unroll=4)
    squares = jnp.sum(squares, axis=0, keepdims=True)
    row = lax.broadcasted_iota(jnp.int32, (8, channels), 0)
    stats = jnp.where(
        row == 0, total, jnp.where(row == 1, squares, jnp.where(row == 2, number, mean))
    )
    mine[...] = stats
    every[0] = stats

    def stat_copy(s):
        return pltpu.make_async_remote_copy(
            src_ref=mine,
            dst_ref=every.at[s],
            send_sem=stat_send.at[s],
            recv_sem=stat_recv.at[s],
            device_id=partner(nx, ny, s),
            device_id_type=MESH,
        )

    each(lambda s: stat_copy(s).start())
    drain(0)
    drain(1)
    each(lambda s: stat_copy(s).wait_recv())
    gathered = every[...]
    average = jnp.sum(gathered[:, 0:1, :], axis=0) / population
    away = gathered[:, 3:4, :] - average[None]
    squares = jnp.sum(gathered[:, 1:2, :] + gathered[:, 2:3, :] * away * away, axis=0)
    out_ref[...] = jnp.where(row == 0, average, squares / population)
    each(lambda s: stat_copy(s).wait_send())


def layer(rim_blocks, outgoing, kernel_map, weights, population):
    nx = lax.axis_size("tx")
    ny = lax.axis_size("ty")
    count = nx * ny
    _, blocks, block_half, channels = outgoing.shape
    rims = rim_blocks.shape[0]
    offsets = weights.shape[0]
    smem = pl.BlockSpec(memory_space=pltpu.SMEM)
    vmem = pl.BlockSpec(memory_space=pltpu.VMEM)
    dma = pltpu.SemaphoreType.DMA
    return pl.pallas_call(
        functools.partial(layer_kernel, nx, ny, population),
        out_shape=(
            jax.ShapeDtypeStruct((blocks * BLOCK, channels), jnp.float32),
            jax.ShapeDtypeStruct((8, channels), jnp.float32),
        ),
        in_specs=[smem, vmem, vmem, vmem],
        out_specs=(vmem, vmem),
        scratch_shapes=[
            pltpu.VMEM((blocks, block_half, channels), jnp.bfloat16),
            pltpu.VMEM((blocks, block_half, channels), jnp.bfloat16),
            pltpu.VMEM((2, rims, block_half, channels), jnp.bfloat16),
            pltpu.VMEM((2, rims, block_half, channels), jnp.bfloat16),
            pltpu.VMEM((blocks, 128), jnp.int32),
            pltpu.SMEM((blocks, 128), jnp.int32),
            pltpu.VMEM((blocks + rims, channels // 2, 128), jnp.float32),
            pltpu.VMEM((2, channels, (offsets + 1) // 2 * channels), jnp.bfloat16),
            pltpu.VMEM((blocks // 4, channels, 256), jnp.float32),
            pltpu.VMEM((blocks // 2, 8, 128), jnp.float32),
            pltpu.VMEM((8, channels), jnp.float32),
            pltpu.VMEM((count, 8, channels), jnp.float32),
            dma((2, count)),
            dma((2, count)),
            dma((2, 4)),
            dma((2, 4)),
            dma((count,)),
            dma((count,)),
            dma(()),
        ],
        compiler_params=pltpu.CompilerParams(
            collective_id=1, has_side_effects=True, vmem_limit_bytes=48 * 1024 * 1024
        ),
    )(rim_blocks, outgoing, kernel_map, weights)


def addresses(target, devices, pair_rows):
    src_count = target.shape[0]
    member = (target[:, None] == jnp.arange(devices, dtype=jnp.int32)[None, :]).astype(jnp.bfloat16)
    run_len = min(512, src_count)
    run_count = src_count // run_len
    member_runs = member.reshape(run_count, run_len, devices)
    lower_ones = (jnp.arange(run_len)[:, None] >= jnp.arange(run_len)[None, :]).astype(jnp.bfloat16)
    inside = jnp.einsum("ij,bjd->bid", lower_ones, member_runs, preferred_element_type=jnp.float32)
    run_totals = inside[:, -1, :]
    before = jnp.cumsum(run_totals, axis=0) - run_totals
    running = (inside + before[:, None, :]).reshape(src_count, devices)
    member_wide = member.astype(jnp.float32)
    placed = jnp.sum((running - 1.0) * member_wide, axis=1).astype(jnp.int32)
    return target * pair_rows + placed


def shards(voxels, owner_tile, rim_blocks, kernel_map, weights, norm_gain, shift_bias):
    devices = lax.axis_size(("tx", "ty"))
    channels = voxels.shape[1]
    tile_rows = kernel_map.shape[2]
    offsets = kernel_map.shape[1]
    pair_rows = tile_rows // devices
    address = addresses(owner_tile[:, 0], devices, pair_rows)
    outgoing = place(address, voxels, tile_rows)
    padded = jnp.pad(kernel_map[0], ((0, 32 - offsets), (0, 0)), constant_values=-1)
    population = float(voxels.shape[0] * devices)
    response, combined = layer(rim_blocks.reshape(-1), outgoing, padded, weights, population)
    average, variance = combined[0], combined[1]
    scaled = norm_gain * (response - average) / jnp.sqrt(variance + 1e-05) + shift_bias
    return jnp.where(response > -5e29, jnp.maximum(scaled, 0.0), 0.0).astype(jnp.bfloat16)


def solution(mesh):
    return jax.shard_map(
        shards,
        mesh=mesh,
        in_specs=(
            P(("tx", "ty"), None),
            P(("tx", "ty"), None),
            P(("tx", "ty"), None, None),
            P(("tx", "ty"), None, None),
            P(),
            P(),
            P(),
        ),
        out_specs=P(("tx", "ty"), None),
        check_vma=False,
    )
```

time: 458 us -> 126 us (0.28)
  matrix products: 175 us -> 0.35 us
  Pallas kernels: 0 us -> 115 us
  local copies, waits for them, and re-layouts: 92.9 us -> 3.16 us
  blocking collectives: 82.5 us -> 0 us
  waiting for transfers between devices: 43.5 us -> 0 us
  other arithmetic: 30.4 us -> 6.43 us
  starting transfers between devices: 19.8 us -> 0 us
  loops' own time: 10.7 us -> 0 us
    dot_general x33 -> x1, matrix products: 175 us -> 0.35 us  [addresses(): jnp.einsum('ij,bjd->bid', lower_ones, member_runs, preferred_element_type...]
    pallas_call x0 -> x2, Pallas kernels: none -> 115 us  [the longest x1 107 us: layer(): pl.pallas_call(functools.partial(layer_kernel, nx, ny, population), out_s...]
    psum x2 -> x0, blocking collectives: 82.5 us -> none  [the longest x1 42.7 us: shards(): average = lax.psum(jnp.sum(response, axis=0), ('tx', 'ty')) / population]
    gather x17 -> x0, local copies, waits for them, and re-layouts: 48.4 us -> none  [the longest x16 46 us: convolve(): fetched = ext_blocks[sources]]
    all_to_all x2 -> x0, waiting for transfers between devices: 38.5 us -> none  [the longest x1 38.5 us: shards(): lax.all_to_all(outgoing.reshape(devices, pair_rows, channels), ('tx', 'ty...]
    dynamic_slice x112 -> x0, local copies, waits for them, and re-layouts: 38.5 us -> none  [the longest x96 28.7 us: shards(): lax.map(convolve, (source_groups, local_groups, valid_groups))]
    all_to_all x2 -> x0, starting transfers between devices: 13.3 us -> none  [the longest x1 7.3 us: shards(): lax.all_to_all(filled.reshape(devices, 1), ('tx', 'ty'), split_axis=0, co...]
    another operation x2 -> x0, loops' own time: 10.7 us -> none  [the longest x1 10.4 us: shards(): lax.map(place_slots, jnp.arange(tile_rows // slot_len, dtype=jnp.int32))]
  transfers between devices with their start and end apart: 6 -> 0, of which waited for: 3 -> 0; matrix products, arithmetic and copies ran while one was open for 16% -> 0% of each run, Pallas kernels for 0% -> 0%
where the time goes in v4:
time: 126 us; the launch traced here: 125 us
  Pallas kernels  115 us (91%)
  other arithmetic  6.43 us (5%)
  local copies, waits for them, and re-layouts  3.16 us (3%)
    pallas_call x1, Pallas kernels, layer(): pl.pallas_call(functools.partial(layer_kernel, nx, ny, population), out_s...  107 us
    pallas_call x1, Pallas kernels, place(): pl.pallas_call(place_kernel, out_shape=jax.ShapeDtypeStruct((2, tile_rows...  8.57 us
    convert_element_type x1, other arithmetic, shards(): jnp.where(response > -5e+29, jnp.maximum(scaled, 0.0), 0.0)  4.59 us

profile of v4, /device:TPU:0, one launch (start us, length us, event | category | flops | bytes accessed | tf_op | source)
XLA Modules:
  0.0 125.5 jit_solution(9014031750804216879)
XLA Ops:
  0.0 0.0 copy-start
  0.0 0.9 reshape.30.rim_ref
  0.9 0.5 broadcast.27
  1.4 1.4 %fusion.5 = (s32[4096]{0:T(1024)S(1)}, s32[4096,1]{0,1:T(1,128)S(1)}) fusion(s32[4096,1]{0,1:T(1,128)} %param.8, s32[]{:T(128)} %broadcast.27), kind=kLoop, calls=%fused_computation.15 | loop fusion | flops 4096 | bytes 49156 | tf_op args[1]
  2.8 0.0 copy-start.1
  2.8 0.3 convolution_bitcast_fusion
  3.2 0.2 fusion.6
  3.4 0.2 multiply_reduce_fusion
  3.6 1.7 %copy.11 = s32[1,27,8192]{2,1,0:T(8,128)S(1)} copy(s32[1,27,8192]{2,0,1:T(1,128)} %param.10) | data formatting | bytes 1769472
  5.3 0.0 copy-start.2
  5.3 0.0 copy-start.3
  5.3 0.1 pad.4.map_ref
  5.4 0.0 copy-done
  5.4 8.6 %shard_map.73.outgoing_ref = bf16[2,128,32,128]{3,2,1,0:T(8,128)(2,1)S(1)} custom-call(s32[4096]{0:T(1024)S(1)} %add.35.address_ref, bf16[4096,128]{1,0:T(8,128)(2,1)S(1)} %copy-done), custom_call_target="tpu_custom_call" | custom-call | tf_op jit(solution)/shard_map/pallas_call | solution.py:52
  14.0 0.0 copy-done.1
  14.0 106.8 %shard_map.74 = (f32[8192,128]{1,0:T(8,128)}, f32[8,128]{1,0:T(8,128)S(1)}) custom-call(s32[64]{0:T(128)S(1)} %reshape.30.rim_ref, bf16[2,128,32,128]{3,2,1,0:T(8,128)(2,1)S(1)} %shard_map.73.outgoing_ref, s32[32,8192]{1,0:T(8,128)S(1)} %pad.4.map_ref, bf16[27,128,128]{2,1,0:T(8,128)(2,1)S(1)} %copy-done.1), custom_call_target="tpu_custom_call" | custom-call | tf_op jit(solution)/shard_map/pallas_call | solution.py:364
  120.8 0.0 copy-done.2
  120.9 0.0 copy-done.3
  120.9 4.6 %select_convert_fusion = bf16[8192,128]{1,0:T(8,128)(2,1)} fusion(f32[8192,128]{1,0:T(8,128)} %get-tuple-element.7, f32[128]{0:T(128)S(1)} %copy-done.2, f32[128]{0:T(128)S(1)} %get-tuple-element.12, f32[128]{0:T(128)S(1)} %get-tuple-element.11, f32[128]{0:T(128)S(1)} %copy-done.3), kind=kLoop, calls=%fused_computation | loop fusion | flops 8388608 | bytes 6293504 | tf_op jit(solution)/shard_map/convert_element_type | solution.py:428
  (5 shorter events, 0.0 us)
Async XLA Ops:
  0.0 5.4 %copy-start = (bf16[4096,128]{1,0:T(8,128)(2,1)S(1)}, bf16[4096,128]{1,0:T(8,128)(2,1)}, u32[]{:S(2)}) copy-start(bf16[4096,128]{1,0:T(8,128)(2,1)} %voxels_ref.1) | copy-start | bytes 3145732
  2.8 11.2 %copy-start.1 = (bf16[27,128,128]{2,1,0:T(8,128)(2,1)S(1)}, bf16[27,128,128]{2,1,0:T(8,128)(2,1)}, u32[]{:S(2)}) copy-start(bf16[27,128,128]{2,1,0:T(8,128)(2,1)} %weights_ref.1) | copy-start | bytes 2654212
  5.3 115.5 %copy-start.2 = (f32[128]{0:T(128)S(1)}, f32[128]{0:T(128)}, u32[]{:S(2)}) copy-start(f32[128]{0:T(128)} %param.13) | copy-start | bytes 1540
  5.3 115.5 %copy-start.3 = (f32[128]{0:T(128)S(1)}, f32[128]{0:T(128)}, u32[]{:S(2)}) copy-start(f32[128]{0:T(128)} %param.12) | copy-start | bytes 1540

commit v5 on v4

--- a/solution.py
+++ b/solution.py
@@ -75,7 +75,7 @@
 
 def layer_kernel(
     nx, ny, population, rim_ref, outgoing_ref, map_ref, weights_ref, resp_ref, out_ref,
-    arrival0, arrival1, staged, rims, found_v, found_s, table, turned, partial, filled, mine, every,
+    arrival0, arrival1, staged, rims, found_v, found_s, spots, table, turned, partial, filled, mine, every,
     send, recv, rim_send, rim_recv, stat_send, stat_recv, local_sem
 ):
     tx = lax.axis_index("tx")
@@ -138,10 +138,11 @@
 
     def send_rims(h):
         def stage(i, carry):
-            staged[h, i] = arrival[h][rim_ref[i]]
+            for number in range(4):
+                staged[h, number * rim + i] = arrival[h][rim_ref[number, i]]
             return carry
 
-        lax.fori_loop(0, 4 * rim, stage, 0)
+        lax.fori_loop(0, rim, stage, 0)
         for number, to, sends, takes in ways:
 
             @pl.when(sends)
@@ -174,8 +175,15 @@
 
     found_v[...] = jnp.zeros_like(found_v)
 
+    second = jnp.where(
+        lax.broadcasted_iota(jnp.int32, (map_ref.shape[0], 128), 1) < BLOCK, 0, BLOCK
+    )
+
     def prepare(c, carry):
-        columns = map_ref[:, pl.ds(pl.multiple_of(c * 128, 128), 128)].T
+        at = pl.ds(pl.multiple_of(c * 128, 128), 128)
+        entries = map_ref[:, at]
+        spots[:, at] = jnp.bitwise_and(entries, BLOCK - 1) + second
+        columns = entries.T
         for i in range(2):
             rows = columns[i * BLOCK : (i + 1) * BLOCK]
             source = jnp.maximum(jnp.max(rows, axis=0, keepdims=True), 0) // BLOCK
@@ -240,7 +248,7 @@
 
     marker = -1e30
 
-    def convolve(h):
+    def convolve(h, first, last):
         def window(w, carry):
             def pick(k, c):
                 b = 2 * (2 * w + c)
@@ -248,8 +256,7 @@
                     return jnp.where(left, table[b], table[b + 1]).astype(jnp.bfloat16)
                 at = pl.ds(pl.multiple_of((2 * w + c) * 128, 128), 128)
                 entry = map_ref[k : k + 1, at]
-                spot = lax.rem(jnp.maximum(entry, 0), BLOCK) + jnp.where(left[:1], 0, BLOCK)
-                spot = jnp.broadcast_to(spot, (half, 128))
+                spot = jnp.broadcast_to(spots[k : k + 1, at], (half, 128))
                 source = jnp.where(left, table[found_s[b, k]], table[found_s[b + 1, k]])
                 taken = jnp.take_along_axis(source, spot, axis=1)
                 return jnp.where(entry >= 0, taken, 0.0).astype(jnp.bfloat16)
@@ -279,7 +286,7 @@
                     resp_ref[pl.ds(pl.multiple_of((2 * w + c) * 128, 128), 128), :] = rows
             return carry
 
-        lax.fori_loop(0, blocks // 4, window, 0)
+        lax.fori_loop(first, last, window, 0)
 
     each(lambda s: copy(0, s).wait_recv())
     send_rims(0)
@@ -287,13 +294,16 @@
     fill_tile(0)
     take_rims(0)
     fill_rims(0)
-    convolve(0)
+    windows = blocks // 4
+    split = windows * 3 // 4
+    convolve(0, 0, split)
     each(lambda s: copy(1, s).wait_recv())
     send_rims(1)
+    convolve(0, split, windows)
     fill_tile(1)
     take_rims(1)
     fill_rims(1)
-    convolve(1)
+    convolve(1, 0, windows)
 
     def rows_of(i):
         value = resp_ref[pl.ds(pl.multiple_of(i * BLOCK, BLOCK), BLOCK), :]
@@ -356,7 +366,7 @@
     ny = lax.axis_size("ty")
     count = nx * ny
     _, blocks, block_half, channels = outgoing.shape
-    rims = rim_blocks.shape[0]
+    rims = rim_blocks.shape[0] * rim_blocks.shape[1]
     offsets = weights.shape[0]
     smem = pl.BlockSpec(memory_space=pltpu.SMEM)
     vmem = pl.BlockSpec(memory_space=pltpu.VMEM)
@@ -376,6 +386,7 @@
             pltpu.VMEM((2, rims, block_half, channels), jnp.bfloat16),
             pltpu.VMEM((blocks, 128), jnp.int32),
             pltpu.SMEM((blocks, 128), jnp.int32),
+            pltpu.VMEM(kernel_map.shape, jnp.int32),
             pltpu.VMEM((blocks + rims, channels // 2, 128), jnp.float32),
             pltpu.VMEM((2, channels, (offsets + 1) // 2 * channels), jnp.bfloat16),
             pltpu.VMEM((blocks // 4, channels, 256), jnp.float32),
@@ -422,7 +433,7 @@
     outgoing = place(address, voxels, tile_rows)
     padded = jnp.pad(kernel_map[0], ((0, 32 - offsets), (0, 0)), constant_values=-1)
     population = float(voxels.shape[0] * devices)
-    response, combined = layer(rim_blocks.reshape(-1), outgoing, padded, weights, population)
+    response, combined = layer(rim_blocks[0], outgoing, padded, weights, population)
     average, variance = combined[0], combined[1]
     scaled = norm_gain * (response - average) / jnp.sqrt(variance + 1e-05) + shift_bias
     return jnp.where(response > -5e29, jnp.maximum(scaled, 0.0), 0.0).astype(jnp.bfloat16)

time: 126 us -> 126 us (level)
  no operation moved by 1% of the time
where the time goes in v5:
time: 126 us; the launch traced here: 125 us
  Pallas kernels  116 us (92%)
  other arithmetic  6.43 us (5%)
  local copies, waits for them, and re-layouts  2.31 us (2%)
    pallas_call x1, Pallas kernels, layer(): pl.pallas_call(functools.partial(layer_kernel, nx, ny, population), out_s...  108 us
    pallas_call x1, Pallas kernels, place(): pl.pallas_call(place_kernel, out_shape=jax.ShapeDtypeStruct((2, tile_rows...  8.57 us
    convert_element_type x1, other arithmetic, shards(): jnp.where(response > -5e+29, jnp.maximum(scaled, 0.0), 0.0)  4.59 us

profile of v5, /device:TPU:0, one launch (start us, length us, event | category | flops | bytes accessed | tf_op | source)
XLA Modules:
  0.0 125.4 jit_solution(14456742429813091270)
XLA Ops:
  0.0 0.0 copy-start
  0.0 0.5 broadcast.27
  0.5 1.4 %fusion.5 = (s32[4096]{0:T(1024)S(1)}, s32[4096,1]{0,1:T(1,128)S(1)}) fusion(s32[4096,1]{0,1:T(1,128)} %param.8, s32[]{:T(128)} %broadcast.27), kind=kLoop, calls=%fused_computation.15 | loop fusion | flops 4096 | bytes 49156 | tf_op args[1]
  1.9 0.0 copy-start.1
  1.9 0.0 copy-start.2
  2.0 0.3 convolution_bitcast_fusion
  2.3 0.2 fusion.6
  2.5 0.2 multiply_reduce_fusion
  2.8 1.7 %copy.11 = s32[1,27,8192]{2,1,0:T(8,128)S(1)} copy(s32[1,27,8192]{2,0,1:T(1,128)} %param.10) | data formatting | bytes 1769472
  4.5 0.0 copy-start.3
  4.5 0.0 copy-start.4
  4.5 0.1 pad.4.map_ref
  4.6 0.0 copy-done
  4.6 8.6 %shard_map.73.outgoing_ref = bf16[2,128,32,128]{3,2,1,0:T(8,128)(2,1)S(1)} custom-call(s32[4096]{0:T(1024)S(1)} %add.35.address_ref, bf16[4096,128]{1,0:T(8,128)(2,1)S(1)} %copy-done), custom_call_target="tpu_custom_call" | custom-call | tf_op jit(solution)/shard_map/pallas_call | solution.py:52
  13.2 0.0 copy-done.1
  13.2 0.0 copy-done.2
  13.2 107.6 %shard_map.74 = (f32[8192,128]{1,0:T(8,128)}, f32[8,128]{1,0:T(8,128)S(1)}) custom-call(s32[4,16]{1,0:T(4,128)S(1)} %bitcast.18, bf16[2,128,32,128]{3,2,1,0:T(8,128)(2,1)S(1)} %shard_map.73.outgoing_ref, s32[32,8192]{1,0:T(8,128)S(1)} %pad.4.map_ref, bf16[27,128,128]{2,1,0:T(8,128)(2,1)S(1)} %copy-done.1), custom_call_target="tpu_custom_call" | custom-call | tf_op jit(solution)/shard_map/pallas_call | solution.py:374
  120.8 0.0 copy-done.3
  120.8 0.0 copy-done.4
  120.8 4.6 %select_convert_fusion = bf16[8192,128]{1,0:T(8,128)(2,1)} fusion(f32[8192,128]{1,0:T(8,128)} %get-tuple-element.7, f32[128]{0:T(128)S(1)} %copy-done.3, f32[128]{0:T(128)S(1)} %get-tuple-element.12, f32[128]{0:T(128)S(1)} %get-tuple-element.11, f32[128]{0:T(128)S(1)} %copy-done.4), kind=kLoop, calls=%fused_computation | loop fusion | flops 8388608 | bytes 6293504 | tf_op jit(solution)/shard_map/convert_element_type | solution.py:439
  (5 shorter events, 0.0 us)
Async XLA Ops:
  0.0 4.6 %copy-start = (bf16[4096,128]{1,0:T(8,128)(2,1)S(1)}, bf16[4096,128]{1,0:T(8,128)(2,1)}, u32[]{:S(2)}) copy-start(bf16[4096,128]{1,0:T(8,128)(2,1)} %voxels_ref.1) | copy-start | bytes 3145732
  1.9 11.2 %copy-start.1 = (bf16[27,128,128]{2,1,0:T(8,128)(2,1)S(1)}, bf16[27,128,128]{2,1,0:T(8,128)(2,1)}, u32[]{:S(2)}) copy-start(bf16[27,128,128]{2,1,0:T(8,128)(2,1)} %weights_ref.1) | copy-start | bytes 2654212
  1.9 11.2 %copy-start.2 = (s32[1,4,16]{2,1,0:T(4,128)S(1)}, s32[1,4,16]{2,1,0:T(4,128)}, u32[]{:S(2)}) copy-start(s32[1,4,16]{2,1,0:T(4,128)} %param.9) | copy-start | bytes 772
  4.5 116.3 %copy-start.3 = (f32[128]{0:T(128)S(1)}, f32[128]{0:T(128)}, u32[]{:S(2)}) copy-start(f32[128]{0:T(128)} %param.13) | copy-start | bytes 1540
  4.5 116.3 %copy-start.4 = (f32[128]{0:T(128)S(1)}, f32[128]{0:T(128)}, u32[]{:S(2)}) copy-start(f32[128]{0:T(128)} %param.12) | copy-start | bytes 1540

commit v6 on v5

--- a/solution.py
+++ b/solution.py
@@ -74,7 +74,7 @@
 
 
 def layer_kernel(
-    nx, ny, population, rim_ref, outgoing_ref, map_ref, weights_ref, resp_ref, out_ref,
+    nx, ny, population, rim_ref, outgoing_ref, map_ref, weights_ref, affine_ref, out_ref, resp_ref,
     arrival0, arrival1, staged, rims, found_v, found_s, spots, table, turned, partial, filled, mine, every,
     send, recv, rim_send, rim_recv, stat_send, stat_recv, local_sem
 ):
@@ -290,12 +290,12 @@
 
     each(lambda s: copy(0, s).wait_recv())
     send_rims(0)
-    each(lambda s: copy(1, s).start())
     fill_tile(0)
     take_rims(0)
+    each(lambda s: copy(1, s).start())
     fill_rims(0)
     windows = blocks // 4
-    split = windows * 3 // 4
+    split = windows * 7 // 8
     convolve(0, 0, split)
     each(lambda s: copy(1, s).wait_recv())
     send_rims(1)
@@ -357,11 +357,21 @@
     average = jnp.sum(gathered[:, 0:1, :], axis=0) / population
     away = gathered[:, 3:4, :] - average[None]
     squares = jnp.sum(gathered[:, 1:2, :] + gathered[:, 2:3, :] * away * away, axis=0)
-    out_ref[...] = jnp.where(row == 0, average, squares / population)
+    gain = affine_ref[0:1, :] * (1.0 / jnp.sqrt(squares / population + 1e-05))
+    bias = affine_ref[1:2, :]
+
+    def finish(i, carry):
+        value, full = rows_of(i)
+        scaled = jnp.maximum((value - average) * gain + bias, 0.0)
+        at = pl.ds(pl.multiple_of(i * BLOCK, BLOCK), BLOCK)
+        out_ref[at, :] = jnp.where(full, scaled, 0.0).astype(jnp.bfloat16)
+        return carry
+
+    lax.fori_loop(0, blocks, finish, 0, unroll=4)
     each(lambda s: stat_copy(s).wait_send())
 
 
-def layer(rim_blocks, outgoing, kernel_map, weights, population):
+def layer(rim_blocks, outgoing, kernel_map, weights, affine, population):
     nx = lax.axis_size("tx")
     ny = lax.axis_size("ty")
     count = nx * ny
@@ -373,13 +383,11 @@
     dma = pltpu.SemaphoreType.DMA
     return pl.pallas_call(
         functools.partial(layer_kernel, nx, ny, population),
-        out_shape=(
-            jax.ShapeDtypeStruct((blocks * BLOCK, channels), jnp.float32),
-            jax.ShapeDtypeStruct((8, channels), jnp.float32),
-        ),
-        in_specs=[smem, vmem, vmem, vmem],
-        out_specs=(vmem, vmem),
+        out_shape=jax.ShapeDtypeStruct((blocks * BLOCK, channels), jnp.bfloat16),
+        in_specs=[smem, vmem, vmem, vmem, vmem],
+        out_specs=vmem,
         scratch_shapes=[
+            pltpu.VMEM((blocks * BLOCK, channels), jnp.float32),
             pltpu.VMEM((blocks, block_half, channels), jnp.bfloat16),
             pltpu.VMEM((blocks, block_half, channels), jnp.bfloat16),
             pltpu.VMEM((2, rims, block_half, channels), jnp.bfloat16),
@@ -404,7 +412,7 @@
         compiler_params=pltpu.CompilerParams(
             collective_id=1, has_side_effects=True, vmem_limit_bytes=48 * 1024 * 1024
         ),
-    )(rim_blocks, outgoing, kernel_map, weights)
+    )(rim_blocks, outgoing, kernel_map, weights, affine)
 
 
 def addresses(target, devices, pair_rows):
@@ -433,10 +441,8 @@
     outgoing = place(address, voxels, tile_rows)
     padded = jnp.pad(kernel_map[0], ((0, 32 - offsets), (0, 0)), constant_values=-1)
     population = float(voxels.shape[0] * devices)
-    response, combined = layer(rim_blocks[0], outgoing, padded, weights, population)
-    average, variance = combined[0], combined[1]
-    scaled = norm_gain * (response - average) / jnp.sqrt(variance + 1e-05) + shift_bias
-    return jnp.where(response > -5e29, jnp.maximum(scaled, 0.0), 0.0).astype(jnp.bfloat16)
+    affine = jnp.stack((norm_gain, shift_bias))
+    return layer(rim_blocks[0], outgoing, padded, weights, affine, population)
 
 
 def solution(mesh):

time: 126 us -> 121 us (0.960)
  other arithmetic: 6.43 us -> 2.58 us
    convert_element_type x1 -> x0, other arithmetic: 4.59 us -> none  [shards(): jnp.where(response > -5e+29, jnp.maximum(scaled, 0.0), 0.0)]
    pallas_call x1, Pallas kernels: 108 us -> 106 us  [layer(): pl.pallas_call(functools.partial(layer_kernel, nx, ny, population), out_s...]
    unnamed x13 -> x12, local copies, waits for them, and re-layouts: 2.24 us -> 2.93 us
where the time goes in v6:
time: 121 us
  Pallas kernels  115 us (95%)
  local copies, waits for them, and re-layouts  3.01 us (2%)
  other arithmetic  2.58 us (2%)
    pallas_call x1, Pallas kernels, layer(): pl.pallas_call(functools.partial(layer_kernel, nx, ny, population), out_s...  106 us
    pallas_call x1, Pallas kernels, place(): pl.pallas_call(place_kernel, out_shape=jax.ShapeDtypeStruct((2, tile_rows...  8.56 us
    unnamed x12, local copies, waits for them, and re-layouts  2.93 us

profile of v6, /device:TPU:0, one launch (start us, length us, event | category | flops | bytes accessed | tf_op | source)
XLA Modules:
  0.0 120.9 jit_solution(9861791595794481693)
XLA Ops:
  0.0 0.0 copy-start.3
  0.0 0.8 pad_maximum_fusion.affine_ref
  0.8 0.5 broadcast.24
  1.3 1.4 %fusion.5 = (s32[4096]{0:T(1024)S(1)}, s32[4096,1]{0,1:T(1,128)S(1)}) fusion(s32[4096,1]{0,1:T(1,128)} %param.8, s32[]{:T(128)} %broadcast.24), kind=kLoop, calls=%fused_computation.13 | loop fusion | flops 4096 | bytes 49156 | tf_op args[1]
  2.7 0.3 convolution_bitcast_fusion
  3.1 0.2 fusion.6
  3.3 0.2 multiply_reduce_fusion
  3.5 0.0 copy-start
  3.5 0.0 copy-done.3
  3.5 0.5 copy.11
  4.1 0.1 pad.4.map_ref
  4.1 0.6 copy-done
  4.7 0.0 copy-start.1
  4.7 0.0 copy-start.2
  4.7 8.6 %shard_map.73.outgoing_ref = bf16[2,128,32,128]{3,2,1,0:T(8,128)(2,1)S(1)} custom-call(s32[4096]{0:T(1024)S(1)} %add.20.address_ref, bf16[4096,128]{1,0:T(8,128)(2,1)S(1)} %copy-done), custom_call_target="tpu_custom_call" | custom-call | tf_op jit(solution)/shard_map/pallas_call | solution.py:52
  13.3 0.0 copy-done.1
  13.3 0.0 copy-done.2
  13.3 106.3 %shard_map.74 = bf16[8192,128]{1,0:T(8,128)(2,1)S(1)} custom-call(s32[4,16]{1,0:T(4,128)S(1)} %bitcast.16, bf16[2,128,32,128]{3,2,1,0:T(8,128)(2,1)S(1)} %shard_map.73.outgoing_ref, s32[32,8192]{1,0:T(8,128)S(1)} %pad.4.map_ref, bf16[27,128,128]{2,1,0:T(8,128)(2,1)S(1)} %copy-done.1, f32[2,128]{1,0:T(2,128)S(1)} %pad_maximum_fusion.affine_ref), custom_call_target="tpu_custom_call" | custom-call | tf_op jit(solution)/shard_map/pallas_call | solution.py:384
  119.6 1.3 %copy.13 = bf16[8192,128]{1,0:T(8,128)(2,1)} copy(bf16[8192,128]{1,0:T(8,128)(2,1)S(1)} %shard_map.74) | data formatting | bytes 4194304
  (4 shorter events, 0.0 us)
Async XLA Ops:
  0.0 3.5 %copy-start.3 = (s32[1,27,8192]{2,0,1:T(1,128)S(1)}, s32[1,27,8192]{2,0,1:T(1,128)}, u32[]{:S(2)}) copy-start(s32[1,27,8192]{2,0,1:T(1,128)} %param.10) | copy-start | bytes 2654212
  3.5 1.2 %copy-start = (bf16[4096,128]{1,0:T(8,128)(2,1)S(1)}, bf16[4096,128]{1,0:T(8,128)(2,1)}, u32[]{:S(2)}) copy-start(bf16[4096,128]{1,0:T(8,128)(2,1)} %voxels_ref.1) | copy-start | bytes 3145732
  4.7 8.6 %copy-start.1 = (bf16[27,128,128]{2,1,0:T(8,128)(2,1)S(1)}, bf16[27,128,128]{2,1,0:T(8,128)(2,1)}, u32[]{:S(2)}) copy-start(bf16[27,128,128]{2,1,0:T(8,128)(2,1)} %weights_ref.1) | copy-start | bytes 2654212
  4.7 8.6 %copy-start.2 = (s32[1,4,16]{2,1,0:T(4,128)S(1)}, s32[1,4,16]{2,1,0:T(4,128)}, u32[]{:S(2)}) copy-start(s32[1,4,16]{2,1,0:T(4,128)} %param.9) | copy-start | bytes 772

commit v7 on v6

--- a/solution.py
+++ b/solution.py
@@ -286,7 +286,7 @@
                     resp_ref[pl.ds(pl.multiple_of((2 * w + c) * 128, 128), 128), :] = rows
             return carry
 
-        lax.fori_loop(first, last, window, 0)
+        lax.fori_loop(first, last, window, 0, unroll=2)
 
     each(lambda s: copy(0, s).wait_recv())
     send_rims(0)

time: 121 us -> 115 us (0.950)
  Pallas kernels: 115 us -> 109 us
    pallas_call x1, Pallas kernels: 106 us -> 101 us  [layer(): pl.pallas_call(functools.partial(layer_kernel, nx, ny, population), out_s...]
where the time goes in v7:
time: 115 us
  Pallas kernels  109 us (95%)
  local copies, waits for them, and re-layouts  3.01 us (3%)
  other arithmetic  2.58 us (2%)
    pallas_call x1, Pallas kernels, layer(): pl.pallas_call(functools.partial(layer_kernel, nx, ny, population), out_s...  101 us
    pallas_call x1, Pallas kernels, place(): pl.pallas_call(place_kernel, out_shape=jax.ShapeDtypeStruct((2, tile_rows...  8.56 us
    unnamed x12, local copies, waits for them, and re-layouts  2.93 us

profile of v7, /device:TPU:0, one launch (start us, length us, event | category | flops | bytes accessed | tf_op | source)
XLA Modules:
  0.0 115.1 jit_solution(5849511915622399267)
XLA Ops:
  0.0 0.0 copy-start.3
  0.0 0.8 pad_maximum_fusion.affine_ref
  0.8 0.5 broadcast.24
  1.3 1.4 %fusion.5 = (s32[4096]{0:T(1024)S(1)}, s32[4096,1]{0,1:T(1,128)S(1)}) fusion(s32[4096,1]{0,1:T(1,128)} %param.8, s32[]{:T(128)} %broadcast.24), kind=kLoop, calls=%fused_computation.13 | loop fusion | flops 4096 | bytes 49156 | tf_op args[1]
  2.7 0.3 convolution_bitcast_fusion
  3.1 0.2 fusion.6
  3.3 0.2 multiply_reduce_fusion
  3.5 0.0 copy-start
  3.5 0.0 copy-done.3
  3.5 0.5 copy.11
  4.1 0.1 pad.4.map_ref
  4.1 0.6 copy-done
  4.7 0.0 copy-start.1
  4.7 0.0 copy-start.2
  4.7 8.6 %shard_map.73.outgoing_ref = bf16[2,128,32,128]{3,2,1,0:T(8,128)(2,1)S(1)} custom-call(s32[4096]{0:T(1024)S(1)} %add.20.address_ref, bf16[4096,128]{1,0:T(8,128)(2,1)S(1)} %copy-done), custom_call_target="tpu_custom_call" | custom-call | tf_op jit(solution)/shard_map/pallas_call | solution.py:52
  13.3 0.0 copy-done.1
  13.3 0.0 copy-done.2
  13.3 100.5 %shard_map.74 = bf16[8192,128]{1,0:T(8,128)(2,1)S(1)} custom-call(s32[4,16]{1,0:T(4,128)S(1)} %bitcast.16, bf16[2,128,32,128]{3,2,1,0:T(8,128)(2,1)S(1)} %shard_map.73.outgoing_ref, s32[32,8192]{1,0:T(8,128)S(1)} %pad.4.map_ref, bf16[27,128,128]{2,1,0:T(8,128)(2,1)S(1)} %copy-done.1, f32[2,128]{1,0:T(2,128)S(1)} %pad_maximum_fusion.affine_ref), custom_call_target="tpu_custom_call" | custom-call | tf_op jit(solution)/shard_map/pallas_call | solution.py:384
  113.8 1.3 %copy.13 = bf16[8192,128]{1,0:T(8,128)(2,1)} copy(bf16[8192,128]{1,0:T(8,128)(2,1)S(1)} %shard_map.74) | data formatting | bytes 4194304
  (4 shorter events, 0.0 us)
Async XLA Ops:
  0.0 3.5 %copy-start.3 = (s32[1,27,8192]{2,0,1:T(1,128)S(1)}, s32[1,27,8192]{2,0,1:T(1,128)}, u32[]{:S(2)}) copy-start(s32[1,27,8192]{2,0,1:T(1,128)} %param.10) | copy-start | bytes 2654212
  3.5 1.2 %copy-start = (bf16[4096,128]{1,0:T(8,128)(2,1)S(1)}, bf16[4096,128]{1,0:T(8,128)(2,1)}, u32[]{:S(2)}) copy-start(bf16[4096,128]{1,0:T(8,128)(2,1)} %voxels_ref.1) | copy-start | bytes 3145732
  4.7 8.6 %copy-start.1 = (bf16[27,128,128]{2,1,0:T(8,128)(2,1)S(1)}, bf16[27,128,128]{2,1,0:T(8,128)(2,1)}, u32[]{:S(2)}) copy-start(bf16[27,128,128]{2,1,0:T(8,128)(2,1)} %weights_ref.1) | copy-start | bytes 2654212
  4.7 8.6 %copy-start.2 = (s32[1,4,16]{2,1,0:T(4,128)S(1)}, s32[1,4,16]{2,1,0:T(4,128)}, u32[]{:S(2)}) copy-start(s32[1,4,16]{2,1,0:T(4,128)} %param.9) | copy-start | bytes 772
